TPU v7x, 32 devices: a whole 2x2x4 slice. The times are simulated.
32 devices in a mesh: heads: 4 (over z), batch: 8 (over y, x, core).
Axes of the slice: x: 2, y: 2, z: 4, core: 2. Of those that a mesh axis runs over, the one named last changes fastest.
Arguments:
- student_rows: bfloat16 [32, 1024, 384], P(('batch', 'heads')), may hold values from -6 to 6
- teacher_rows: bfloat16 [32, 1024, 768], P(('batch', 'heads')), may hold values from -6 to 6
- valid_length: int32 [32], P('batch'), may hold values from 512 to 1024, as said below
- split_point: int32 [32], P('batch'), may hold values from 2 to 1022, as said below
- project_five: bfloat16 [384, 3, 384], P(None, None, 'heads'), may hold values from -0.3125 to 0.3125
- bias_five: bfloat16 [2, 384], P(None, 'heads'), may hold values from -3 to 3
- output_five: bfloat16 [384, 384], P('heads'), may hold values from -1.25 to 1.25
- branch_bias: float32 [2, 384], replicated, may hold values from -2 to 2
- norm_gain: float32 [2, 384], replicated, may hold values from 0.5 to 1.5
- norm_bias: float32 [2, 384], replicated, may hold values from -2 to 2
- widen_weight: bfloat16 [384, 1536], P(None, 'heads'), may hold values from -0.3125 to 0.3125
- widen_bias: bfloat16 [1536], P('heads'), may hold values from -3 to 3
- narrow_weight: bfloat16 [1536, 384], P('heads'), may hold values from -0.15625 to 0.15625
- project_six: bfloat16 [384, 3, 384], P(None, None, 'heads'), may hold values from -0.3125 to 0.3125
- bias_six: bfloat16 [2, 384], P(None, 'heads'), may hold values from -3 to 3
- teacher_project: bfloat16 [768, 3, 768], P(None, None, 'heads'), may hold values from -0.21875 to 0.21875
- teacher_bias: bfloat16 [2, 768], P(None, 'heads'), may hold values from -3 to 3
Outputs:
- block_out: bfloat16 [32, 1024, 384], P(('batch', 'heads'))
- grad_in: float32 [32, 1024, 384], P(('batch', 'heads'))
- grad_project_five: float32 [384, 3, 384], P(None, None, 'heads')
- grad_bias_five: float32 [2, 384], P(None, 'heads')
- grad_output_five: float32 [384, 384], P('heads')
- grad_branch_bias: float32 [2, 384], replicated
- grad_norm_gain: float32 [2, 384], replicated
- grad_norm_bias: float32 [2, 384], replicated
- grad_widen_weight: float32 [384, 1536], P(None, 'heads')
- grad_widen_bias: float32 [1536], P('heads')
- grad_narrow_weight: float32 [1536, 384], P('heads')
- grad_project_six: float32 [384, 3, 384], P(None, None, 'heads')
- grad_bias_six: float32 [2, 384], P(None, 'heads')
- summary: float32 [4], replicated
Inputs may be any that keep to these rules, and one draw needn't show every extreme that they name: `valid_length`: in each group of 4 sequences that share an index of batch, one has length 1024; one sequence of the whole batch has length 512. 2 <= split_point <= valid_length - 2 for each sequence.
All inputs are finite; a program needn't handle non-finite values.
Results may differ from a plain program's by a relative error of at most 0.033.
Values may be sent and summed in bfloat16 or wider, within the bound.
No kernel may reach another device: no remote copies, remote signals or barrier semaphores. Data moves between devices by JAX's collectives and lax.ppermute only.
A program may use at most 192 MiB of HBM per device.

v0:
```python
import functools
import math

import jax
import jax.numpy as jnp
from jax import lax
from jax.experimental import pallas as pl
from jax.experimental.pallas import tpu as pltpu
from jax.sharding import PartitionSpec as P

D = 384
HEADS = 12
HEAD_DIM = 32
TEACHER_HEAD_DIM = 64
PART = 3
TILE = 512
MID_ROWS = 2 * D + 128
STRIP = 16
NORM_EPS = 1e-12
MASKED = -1e30
SAFE = 64.0
LN2 = math.log(2.0)
STUDENT_SCALE = 1.0 / math.sqrt(HEAD_DIM)
STUDENT_LOG = math.log2(math.e) / math.sqrt(HEAD_DIM)
TEACHER_LOG = math.log2(math.e) / math.sqrt(TEACHER_HEAD_DIM)
VMEM = 56 * 2**20

f32 = jnp.float32
bf16 = jnp.bfloat16

NN = (((1,), (0,)), ((), ()))
NT = (((1,), (1,)), ((), ()))
TN = (((0,), (0,)), ((), ()))


def dot(left, right, dims=NN):
    return lax.dot_general(left, right, dims, preferred_element_type=f32)


def lanes(shape):
    return lax.broadcasted_iota(jnp.int32, shape, 1)


def wide_rows(rows):
    return jnp.concatenate([rows, jnp.zeros((rows.shape[0], 128 - rows.shape[1]), rows.dtype)], axis=1)


def in_head(lane, head, size=HEAD_DIM):
    return (lane >= head * size) & (lane < (head + 1) * size)


def split_terms(rows, head, size, extra):
    inside = in_head(lanes(rows.shape), head, size)
    high = rows.astype(bf16).astype(f32)
    first = jnp.where(inside, high, extra).astype(bf16)
    second = jnp.where(inside, rows - high, 0.0).astype(bf16)
    return jnp.concatenate([first, second], axis=1)


def own_number(ref):
    return ref[lax.axis_index("heads")]


def key_bias(rows, length):
    position = lax.broadcasted_iota(jnp.int32, (rows, 1), 0)
    return jnp.where(position < length, 0.0, MASKED)


def fold(tile, combine):
    total = tile[:, :128]
    for column in range(128, tile.shape[1], 128):
        total = combine(total, tile[:, column : column + 128])
    return total


def row_sum(tile):
    return jnp.sum(fold(tile, jnp.add), axis=1, keepdims=True)


def weave(first, second):
    done = 0
    for index, step in enumerate(second):
        while done < len(first) and done * len(second) < len(first) * (index + 1):
            first[done]()
            done += 1
        step()
    for step in first[done:]:
        step()


def step_place(step, tile, per_head):
    head = step // per_head
    return head, pl.ds(pl.multiple_of(lax.rem(step, per_head) * tile, tile), tile)


def run_pipeline(steps, logits, vector, back, enter=None):
    def stage(step, slot, before, after, second=False):
        if enter is not None:
            enter(step, slot, not before, second)
        ahead = logits(step + 1, 1 - slot) if after else []
        behind = back(step - 1, 1 - slot) if before else []
        weave(ahead + behind, vector(step, slot))

    for chunk in logits(jnp.int32(0), 0):
        chunk()
    stage(jnp.int32(0), 0, False, True)
    stage(jnp.int32(1), 1, True, True, second=True)

    def pair(index, carry):
        stage(2 * index + 2, 0, True, True)
        stage(2 * index + 3, 1, True, True)
        return carry

    lax.fori_loop(0, (steps - 4) // 2, pair, 0)
    stage(jnp.int32(steps - 2), 0, True, True)
    stage(jnp.int32(steps - 1), 1, True, False)
    for chunk in back(jnp.int32(steps - 1), 1):
        chunk()


def project_part(x, w_ref, index, bias):
    flat = dot(x, w_ref[index * 96 : (index + 1) * 96, :], NT)
    if bias is not None:
        flat = flat + bias
    return wide_rows(flat).astype(bf16)


def attend_forward_kernel(
    length_ref, x_ref, w_ref, q_ref, k_ref, v_ref, e_hbm, r_ref, o_ref, lhs, rhs, mixer, zs0, zs1, es0, es1, sems
):
    share = pl.program_id(0)
    w_ref, q_ref, k_ref, v_ref, r_ref, o_ref = (t.at[0] for t in (w_ref, q_ref, k_ref, v_ref, r_ref, o_ref))
    zs, es = (zs0, zs1), (es0, es1)
    rows = x_ref.shape[0]
    tile = zs0.shape[0]
    per_head = rows // tile
    steps = PART * per_head
    x = x_ref[...]
    small = w_ref[288:304, :].astype(f32)
    q = project_part(x, w_ref, 0, small[0:1, :96])
    k = project_part(x, w_ref, 1, None)
    v = project_part(x, w_ref, 2, small[1:2, :96])
    q_ref[...] = q
    k_ref[...] = k
    v_ref[...] = v
    lane = lanes((rows, 128))
    one = jnp.where(lane == 96, 1.0, 0.0)
    for head in range(PART):
        lhs[head] = jnp.where(in_head(lane, head), q.astype(f32), one).astype(bf16)
    rhs[...] = jnp.where(lane == 96, key_bias(rows, own_number(length_ref)), k.astype(f32)).astype(bf16)
    mixer[...] = jnp.where(lane == 96, 1.0, v.astype(f32)).astype(bf16)
    o_ref[...] = jnp.zeros_like(o_ref)
    r_ref[...] = jnp.zeros_like(r_ref)

    def out_copy(step, slot):
        head, span = step_place(step, tile, per_head)
        return pltpu.make_async_copy(es[slot], e_hbm.at[share, head, span], sems.at[slot])

    def logits(step, slot):
        head, span = step_place(step, tile, per_head)

        def chunk(start):
            zs[slot][:, start : start + 256] = dot(lhs[head, span, :], rhs[start : start + 256, :], NT)

        return [functools.partial(chunk, start) for start in range(0, rows, 256)]

    def vector(step, slot):
        def strip(start):
            z = zs[slot][start : start + STRIP, :]
            highest = jnp.max(fold(z, jnp.maximum), axis=1, keepdims=True)
            es[slot][start : start + STRIP, :] = jnp.exp2((z - highest) * STUDENT_LOG).astype(bf16)

        return [functools.partial(strip, start) for start in range(0, tile, STRIP)]

    def back(step, slot):
        head, span = step_place(step, tile, per_head)

        sums = []

        def part(start):
            sums.append(dot(es[slot][:, start : start + 256], mixer[start : start + 256, :]))

        def mix():
            mixed = functools.reduce(jnp.add, sums)
            inverse = 1.0 / mixed[:, 96:97]
            inside = in_head(lanes(mixed.shape), head)
            o_ref[span, :] = jnp.where(inside, mixed * inverse, o_ref[span, :].astype(f32)).astype(bf16)
            r_ref[span, :] = jnp.where(inside, inverse, r_ref[span, :])

        return [functools.partial(part, start) for start in range(0, rows, 256)] + [mix]

    def enter(step, slot, first, second):
        if not first:
            out_copy(step - 1, 1 - slot).start()
        if not (first or second):
            out_copy(step - 2, slot).wait()

    run_pipeline(steps, logits, vector, back, enter)
    out_copy(jnp.int32(steps - 1), 1).start()
    out_copy(jnp.int32(steps - 2), 0).wait()
    out_copy(jnp.int32(steps - 1), 1).wait()


def whole(shape):
    return pl.BlockSpec(shape, lambda *_: (0,) * len(shape))


SMEM = pl.BlockSpec(memory_space=pltpu.SMEM)
ANY = pl.BlockSpec(memory_space=pl.ANY)


def cost(micros):
    return pl.CostEstimate(flops=int(micros * 0.04e9), bytes_accessed=1024, transcendentals=0)


def attend_forward(length, x, w):
    rows, count = x.shape[0], w.shape[0]
    tile = min(TILE, rows // 2)
    narrow = jax.ShapeDtypeStruct((count, rows, 128), bf16)

    def share(shape):
        return pl.BlockSpec((1,) + shape, lambda s: (s,) + (0,) * len(shape))

    row = share((rows, 128))
    return pl.pallas_call(
        attend_forward_kernel,
        grid=(count,),
        in_specs=[SMEM, whole(x.shape), share(w.shape[1:])],
        out_specs=[row] * 3 + [ANY] + [row] * 2,
        out_shape=[
            narrow, narrow, narrow, jax.ShapeDtypeStruct((count, PART, rows, rows), bf16),
            jax.ShapeDtypeStruct((count, rows, 128), f32), narrow,
        ],
        scratch_shapes=[
            pltpu.VMEM((PART, rows, 128), bf16),
            pltpu.VMEM((rows, 128), bf16),
            pltpu.VMEM((rows, 128), bf16),
            pltpu.VMEM((tile, rows), f32),
            pltpu.VMEM((tile, rows), f32),
            pltpu.VMEM((tile, rows), bf16),
            pltpu.VMEM((tile, rows), bf16),
            pltpu.SemaphoreType.DMA((2,)),
        ],
        compiler_params=pltpu.CompilerParams(vmem_limit_bytes=VMEM),
        cost_estimate=cost(9 * count),
        name="attend_forward",
    )(length, x, w)


def attend_backward_kernel(
    q_ref, k_ref, v_ref, e_hbm, r_ref, a_ref, d_ref, x_hbm, w_hbm, acc_hbm, tail_ref, g_ref, in_ref,
    lhs, rhs, keys, qt, dt, zs0, zs1, gs0, gs1, dq, dkt, dvt, e_all, x_ref, w_ref, acc_ref, sems, late, *, share,
):
    q_ref, k_ref, v_ref, r_ref, a_ref = (t.at[0] for t in (q_ref, k_ref, v_ref, r_ref, a_ref))
    rows = q_ref.shape[0]
    zs, gs = (zs0, zs1), (gs0, gs1)
    tile = zs0.shape[0]
    per_head = rows // tile
    steps = PART * per_head

    def in_copy(step):
        head, span = step_place(step, tile, per_head)
        return pltpu.make_async_copy(e_hbm.at[share, head, span], e_all.at[head, span], sems.at[step])

    def begin(step, carry):
        in_copy(step).start()
        return carry

    lax.fori_loop(0, steps, begin, 0)
    late_copies = [
        pltpu.make_async_copy(source, target, late.at[index])
        for index, (source, target) in enumerate(((x_hbm, x_ref), (w_hbm.at[share], w_ref), (acc_hbm, acc_ref)))
    ]
    for copy in late_copies:
        copy.start()
    lane = lanes((rows, 128))
    grads = r_ref[...] * d_ref[...].astype(f32)
    shifts = grads * a_ref[...].astype(f32)
    k = k_ref[...].astype(f32)
    for head in range(PART):
        inside = in_head(lane, head)
        shift = -jnp.sum(jnp.where(inside, shifts, 0.0), axis=1, keepdims=True)
        high = shift.astype(bf16).astype(f32)
        lhs[head] = split_terms(
            grads, head, HEAD_DIM, jnp.where(lane == 96, high, jnp.where(lane == 97, shift - high, 0.0))
        )
        keys[head] = jnp.where(inside, k, 0.0).astype(bf16)
    rhs[:, :128] = jnp.where((lane == 96) | (lane == 97), 1.0, v_ref[...].astype(f32)).astype(bf16)
    rhs[:, 128:] = v_ref[...]
    qt[...] = q_ref[...].T
    dt[...] = grads.astype(bf16).T
    dq[...] = jnp.zeros_like(dq)
    dkt[...] = jnp.zeros_like(dkt)
    dvt[...] = jnp.zeros_like(dvt)

    def logits(step, slot):
        head, span = step_place(step, tile, per_head)

        def chunk(start):
            zs[slot][:, start : start + 256] = dot(lhs[head, span, :], rhs[start : start + 256, :], NT)

        return [functools.partial(chunk, start) for start in range(0, rows, 256)]

    def vector(step, slot):
        head, span = step_place(step, tile, per_head)
        base = lax.rem(step, per_head) * tile

        def strip(start):
            here = pl.ds(pl.multiple_of(base + start, STRIP), STRIP)
            weights = e_all[head, here, :].astype(f32)
            gs[slot][start : start + STRIP, :] = (weights * zs[slot][start : start + STRIP, :]).astype(bf16)

        return [functools.partial(strip, start) for start in range(0, tile, STRIP)]

    def back(step, slot):
        head, span = step_place(step, tile, per_head)
        own = pl.ds(pl.multiple_of(head * HEAD_DIM, HEAD_DIM), HEAD_DIM)

        def first():
            dq[span, :] += dot(gs[slot][...], keys[head])

        def second(start):
            part = slice(start, start + 256)
            dkt[own, part] += dot(qt[own, span], gs[slot][:, part])

        def third(start):
            part = slice(start, start + 256)
            dvt[own, part] += dot(dt[own, span], e_all[head, span, part])

        starts = range(0, rows, 256)
        return [first] + [functools.partial(second, s) for s in starts] + [functools.partial(third, s) for s in starts]

    run_pipeline(steps, logits, vector, back, lambda step, slot, first, second: in_copy(step).wait())
    for copy in late_copies:
        copy.wait()
    grads = (
        (dq[...] * STUDENT_SCALE).astype(bf16),
        (dkt[...] * STUDENT_SCALE).T.astype(bf16),
        dvt[...].T.astype(bf16),
    )
    weight_grads(grads, x_ref[...], g_ref, tail_ref[:16, :].astype(f32), tail_ref[16:, :].astype(f32))
    in_ref[...] = acc_ref[...] + spread(grads, w_ref)


def weight_grads(grads, x, g_ref, tail_high=0.0, tail_low=0.0):
    for index, grad in enumerate(grads):
        g_ref[index * 96 : (index + 1) * 96, :] = dot(grad, x, TN)[:96].astype(bf16)
    ones = jnp.ones((16, x.shape[0]), bf16)
    row = lax.broadcasted_iota(jnp.int32, (16, 128), 0)
    sums = jnp.where(row == 0, dot(ones, grads[0]), jnp.where(row == 1, dot(ones, grads[2]), 0.0))
    sums = jnp.concatenate([sums, jnp.zeros((16, x.shape[1] - 128), f32)], axis=1) + tail_high
    high = sums.astype(bf16).astype(f32)
    g_ref[288:304, :] = high.astype(bf16)
    g_ref[304:320, :] = (sums - high + tail_low).astype(bf16)


def spread(grads, w_ref):
    total = None
    for index, grad in enumerate(grads):
        term = dot(grad[:, :96], w_ref[index * 96 : (index + 1) * 96, :])
        total = term if total is None else total + term
    return total


def attend_backward(share, q, k, v, e, r, attended, d_attended, x, w, grad_in, tail):
    rows = x.shape[0]
    tile = min(TILE, rows // 2)
    row = pl.BlockSpec((1, rows, 128), lambda i: (share, 0, 0))
    return pl.pallas_call(
        functools.partial(attend_backward_kernel, share=share),
        grid=(1,),
        in_specs=[row, row, row, ANY, row, row, whole((rows, 128)), ANY, ANY, ANY, whole(tail.shape)],
        out_specs=[whole((320, x.shape[1])), whole(x.shape)],
        out_shape=[jax.ShapeDtypeStruct((320, x.shape[1]), bf16), jax.ShapeDtypeStruct(x.shape, f32)],
        scratch_shapes=[
            pltpu.VMEM((PART, rows, 256), bf16),
            pltpu.VMEM((rows, 256), bf16),
            pltpu.VMEM((PART, rows, 128), bf16),
            pltpu.VMEM((128, rows), bf16),
            pltpu.VMEM((128, rows), bf16),
            pltpu.VMEM((tile, rows), f32),
            pltpu.VMEM((tile, rows), f32),
            pltpu.VMEM((tile, rows), bf16),
            pltpu.VMEM((tile, rows), bf16),
            pltpu.VMEM((rows, 128), f32),
            pltpu.VMEM((128, rows), f32),
            pltpu.VMEM((128, rows), f32),
            pltpu.VMEM((PART, rows, rows), bf16),
            pltpu.VMEM(x.shape, bf16),
            pltpu.VMEM(w.shape[1:], bf16),
            pltpu.VMEM(x.shape, f32),
            pltpu.SemaphoreType.DMA((PART * (rows // tile),)),
            pltpu.SemaphoreType.DMA((3,)),
        ],
        compiler_params=pltpu.CompilerParams(vmem_limit_bytes=VMEM),
        cost_estimate=cost(10),
        name="attend_backward",
    )(q, k, v, e, r, attended, d_attended, x, w, grad_in, tail)


def relation_kernel(
    length_ref, split_ref, block_ref, teacher_ref, own_ref, packed_ref, small_ref, d_ref, g_ref, kl_ref, pack, ls, rs, lt, rt, keys, left_t, zs, zt, gs, left_sum, right_t, es_all, et_all, weight, grads_s,
    *, all_rows,
):
    rows = block_ref.shape[0]
    tile = zs.shape[1]
    per_head = rows // tile
    steps = PART * per_head
    length, split = own_number(length_ref), own_number(split_ref)
    block = block_ref[...]
    teacher = teacher_ref[...]
    @pl.when(pl.program_id(0) == 0)
    def _():
        pack[...] = own_ref[...]

    @pl.when(pl.program_id(0) > 0)
    def _():
        unpack(packed_ref, 0, pack, MID_ROWS)

    w_ref, g_ref = pack, g_ref.at[0]
    small = small_ref[0].astype(f32)
    lane = lanes((rows, 128))
    position = lax.broadcasted_iota(jnp.int32, (rows, 1), 0)
    bias = key_bias(rows, length)

    @pl.when(pl.program_id(0) == 0)
    def _():
        counted = (position < length) & (position != 0) & (position != split - 1) & (position != length - 1)
        share = 1.0 / ((length - 3).astype(f32) * float(all_rows))
        weight[...] = jnp.where(counted, share, 0.0)
        kl_ref[...] = jnp.zeros_like(kl_ref)
        d_ref[...] = jnp.zeros_like(d_ref)

    def teacher_part(index, b):
        start = 288 + index * 192
        flat = dot(teacher[:, :D], pack[start : start + 192, :], NT)
        flat = flat + dot(teacher[:, D:], pack[start + 576 : start + 768, :], NT)
        if b is not None:
            flat = flat + b
        flat = flat.astype(bf16)
        return flat[:, :128], wide_rows(flat[:, 128:])

    def largest(rows_low, size, blocks):
        square = rows_low.astype(f32)
        square = (square * square).astype(bf16)
        feature = lax.broadcasted_iota(jnp.int32, (128, 128), 0) // size
        same = feature == lanes((128, 128)) // size
        return jnp.max(dot(square, jnp.where(same, 1.0, 0.0).astype(bf16)), axis=0, keepdims=True)

    def relate(left, right, t_left, t_right, symmetric):
        left_sum[...] = jnp.zeros_like(left_sum)
        right_t[...] = jnp.zeros_like(right_t)
        left_t[...] = left.T
        left_wide = left.astype(f32) * STUDENT_LOG
        right_wide = right.astype(f32)
        one = jnp.where(lane == 96, 1.0, 0.0)
        if symmetric:
            one = jnp.where(lane == 97, bias, one)
        first = jnp.where(lane == 96, bias, right_wide)
        if symmetric:
            first = jnp.where(lane == 97, 1.0, first)
        rs[:, :128] = first.astype(bf16)
        rs[:, 128:] = right
        for head in range(PART):
            ls[head] = split_terms(left_wide, head, HEAD_DIM, one)
            keys[head] = jnp.where(in_head(lane, head), right_wide, 0.0).astype(bf16)
            own = head % 2
            spare = (1 - own) * TEACHER_HEAD_DIM
            one_t = jnp.where(lane == spare, 1.0, 0.0)
            wide_t = t_right[head // 2].astype(f32)
            first_t = jnp.where(lane == spare, bias, wide_t)
            if symmetric:
                one_t = jnp.where(lane == spare + 1, bias, one_t)
                first_t = jnp.where(lane == spare + 1, 1.0, first_t)
            lt[head] = split_terms(t_left[head // 2].astype(f32) * TEACHER_LOG, own, TEACHER_HEAD_DIM, one_t)
            rt[head, :, :128] = first_t.astype(bf16)
            rt[head, :, 128:] = t_right[head // 2]
        student_bound = largest(left, HEAD_DIM, 4) * largest(right, HEAD_DIM, 4) * STUDENT_LOG**2
        bound = jnp.max(student_bound)
        for part in range(2):
            t_bound = largest(t_left[part], TEACHER_HEAD_DIM, 2) * largest(t_right[part], TEACHER_HEAD_DIM, 2)
            bound = jnp.maximum(bound, jnp.max(t_bound * TEACHER_LOG**2))
        near = bound < SAFE * SAFE

        @pl.when(near)
        def _():
            if symmetric:
                symmetric_pass()
            else:
                plain_pass()

        @pl.when(jnp.logical_not(near))
        def _():
            for head in range(PART):
                own = head % 2
                spare = (1 - own) * TEACHER_HEAD_DIM
                ls[head] = split_terms(left.astype(f32), head, HEAD_DIM, jnp.where(lane == 96, 1.0, 0.0))
                lt[head] = split_terms(
                    t_left[head // 2].astype(f32), own, TEACHER_HEAD_DIM, jnp.where(lane == spare, 1.0, 0.0)
                )
            shifted_pass()

    def plain_pass():
        def logits(step, slot):
            head, span = step_place(step, tile, per_head)

            def student(start):
                zs[slot, :, start : start + 256] = dot(ls[head, span, :], rs[start : start + 256, :], NT)

            def taught(start):
                zt[slot, :, start : start + 256] = dot(lt[head, span, :], rt[head, start : start + 256, :], NT)

            chunks = []
            for start in range(0, rows, 256):
                chunks += [functools.partial(student, start), functools.partial(taught, start)]
            return chunks

        def vector(step, slot):
            base = lax.rem(step, per_head) * tile

            def strip(start):
                here = pl.ds(pl.multiple_of(base + start, STRIP), STRIP)
                student = zs[slot, start : start + STRIP, :]
                taught = zt[slot, start : start + STRIP, :]
                es = jnp.exp2(student)
                et = jnp.exp2(taught)
                sum_s = row_sum(es)
                sum_t = row_sum(et)
                cross = row_sum(et * (taught - student))
                w = weight[here, :]
                inverse = 1.0 / sum_t
                kl_ref[here, :] += w * (LN2 * cross * inverse + jnp.log(sum_s) - jnp.log(sum_t))
                gs[slot, start : start + STRIP, :] = (es * (w / sum_s) - et * (w * inverse)).astype(bf16)

            return [functools.partial(strip, start) for start in range(0, tile, STRIP)]

        run_pipeline(steps, logits, vector, grad_products)

    def grad_products(step, slot):
        head, span = step_place(step, tile, per_head)
        own = pl.ds(pl.multiple_of(head * HEAD_DIM, HEAD_DIM), HEAD_DIM)

        def first():
            left_sum[span, :] += dot(gs[slot], keys[head])

        def second(start):
            part = slice(start, start + 256)
            right_t[own, part] += dot(left_t[own, span], gs[slot, :, part])

        return [first] + [functools.partial(second, start) for start in range(0, rows, 256)]

    def shifted_pass():
        def one(step, carry):
            head, span = step_place(step, tile, per_head)
            student = dot(ls[head, span, :], rs[...], NT)
            student = (student - jnp.max(student, axis=1, keepdims=True)) * STUDENT_LOG
            taught = dot(lt[head, span, :], rt[head], NT)
            taught = (taught - jnp.max(taught, axis=1, keepdims=True)) * TEACHER_LOG
            es = jnp.exp2(student)
            et = jnp.exp2(taught)
            sum_s = jnp.sum(es, axis=1, keepdims=True)
            sum_t = jnp.sum(et, axis=1, keepdims=True)
            cross = jnp.sum(et * (taught - student), axis=1, keepdims=True)
            w = weight[span, :]
            row = LN2 * cross / sum_t + jnp.log(sum_s) - jnp.log(sum_t)
            kl_ref[span, :] += jnp.where(w > 0.0, w * row, 0.0)
            gs[0] = (es * (w / sum_s) - et * (w / sum_t)).astype(bf16)
            for chunk in grad_products(step, 0):
                chunk()
            return carry

        lax.fori_loop(0, steps, one, 0)

    def symmetric_pass():
        size = min(256, rows)
        count = rows // size

        def column(row):
            return jnp.broadcast_to(row, (128, size)).T[:, :1]

        def row_of(value):
            return jnp.broadcast_to(value, (size, 128)).T[:1, :]

        def one_head(head, carry):
            own = pl.ds(pl.multiple_of(head * HEAD_DIM, HEAD_DIM), HEAD_DIM)
            by_row = []
            by_column = [[jnp.zeros((1, size), f32)] * 3 for _ in range(count)]
            for i in range(count):
                here = slice(i * size, (i + 1) * size)
                after = slice(i * size, rows)
                student = dot(ls[head, here, :], rs[after, :], NT)
                taught = dot(lt[head, here, :], rt[head, after, :], NT)
                es = jnp.exp2(student)
                et = jnp.exp2(taught)
                cross = et * (taught - student)
                es_all[here, after] = es
                et_all[here, after] = et
                by_row.append([row_sum(t) for t in (es, et, cross)])
                for j in range(i + 1, count):
                    part = slice((j - i) * size, (j - i + 1) * size)
                    by_column[j] = [
                        c + jnp.sum(t[:, part], axis=0, keepdims=True)
                        for c, t in zip(by_column[j], (es, et, cross))
                    ]
            a, b = [], []
            for i in range(count):
                here = slice(i * size, (i + 1) * size)
                sum_s, sum_t, cross = (r + column(c) for r, c in zip(by_row[i], by_column[i]))
                w = weight[here, :]
                sum_s = jnp.where(w > 0.0, sum_s, 1.0)
                sum_t = jnp.where(w > 0.0, sum_t, 1.0)
                inverse = 1.0 / sum_t
                kl_ref[here, :] += w * (LN2 * cross * inverse + jnp.log(sum_s) - jnp.log(sum_t))
                a.append(w / sum_s)
                b.append(w * inverse)
            a_row = jnp.concatenate([row_of(t) for t in a], axis=1)
            b_row = jnp.concatenate([row_of(t) for t in b], axis=1)
            for i in range(count):
                here = slice(i * size, (i + 1) * size)
                after = slice(i * size, rows)
                both = es_all[here, after] * (a[i] + a_row[:, after])
                both = (both - et_all[here, after] * (b[i] + b_row[:, after])).astype(bf16)
                left_sum[here, :] += dot(both, keys[head, after, :])
                if i + 1 < count:
                    right_t[own, (i + 1) * size :] += dot(left_t[own, here], both[:, size:])
            return carry

        lax.fori_loop(0, PART, one_head, 0)

    q = project_part(block, w_ref, 0, small[2:3, :96])
    k = project_part(block, w_ref, 1, None)
    tq = teacher_part(0, small[5:6, :192])
    tk = teacher_part(1, None)
    relate(q, k, tq, tk, False)
    grads_s[0] = (left_sum[...] * STUDENT_SCALE).astype(bf16)
    grads_s[1] = (right_t[...] * STUDENT_SCALE).T.astype(bf16)
    v = project_part(block, w_ref, 2, small[3:4, :96])
    tv = teacher_part(2, small[6:7, :192])
    relate(v, v, tv, tv, True)
    grads_s[2] = ((left_sum[...] + right_t[...].T) * STUDENT_SCALE).astype(bf16)
    grads = tuple(grads_s[i] for i in range(3))
    weight_grads(grads, block, g_ref)
    d_ref[...] += spread(grads, w_ref)


def part_rows(rows, batch):
    return -(-rows // (16 * batch)) * 16


def unpack(packed_ref, share, target, before=0):
    rows, batch = target.shape[0], packed_ref.shape[0]
    part = part_rows(rows, batch)
    offset = part_rows(before, batch)
    for start in range(0, rows, part):
        size = min(part, rows - start)
        target[start : start + size, :] = packed_ref[start // part, share, offset : offset + size, :]


def relations(length, split, block, teacher, own, packed, small, all_rows):
    rows = block.shape[0]
    tile = min(TILE, rows // 2)
    shares = small.shape[0]

    def share(shape):
        return pl.BlockSpec((1,) + shape[1:], lambda s: (s,) + (0,) * (len(shape) - 1))

    place = pl.BlockSpec((packed.shape[0], 1) + packed.shape[2:], lambda s: (0, jnp.maximum(s - 1, 0), 0, 0))
    return pl.pallas_call(
        functools.partial(relation_kernel, all_rows=all_rows),
        grid=(shares,),
        in_specs=[
            SMEM, SMEM, whole(block.shape), whole(teacher.shape), whole(own.shape), place, share(small.shape),
        ],
        out_specs=[whole(block.shape), share((shares, 320, D)), whole((rows, 1))],
        out_shape=[
            jax.ShapeDtypeStruct(block.shape, f32),
            jax.ShapeDtypeStruct((shares, 320, D), bf16),
            jax.ShapeDtypeStruct((rows, 1), f32),
        ],
        scratch_shapes=[
            pltpu.VMEM((1440, D), bf16),
            pltpu.VMEM((PART, rows, 256), bf16),
            pltpu.VMEM((rows, 256), bf16),
            pltpu.VMEM((PART, rows, 256), bf16),
            pltpu.VMEM((PART, rows, 256), bf16),
            pltpu.VMEM((PART, rows, 128), bf16),
            pltpu.VMEM((128, rows), bf16),
            pltpu.VMEM((2, tile, rows), f32),
            pltpu.VMEM((2, tile, rows), f32),
            pltpu.VMEM((2, tile, rows), bf16),
            pltpu.VMEM((rows, 128), f32),
            pltpu.VMEM((128, rows), f32),
            pltpu.VMEM((rows, rows), f32),
            pltpu.VMEM((rows, rows), f32),
            pltpu.VMEM((rows, 1), f32),
            pltpu.VMEM((3, rows, 128), bf16),
        ],
        compiler_params=pltpu.CompilerParams(vmem_limit_bytes=VMEM),
        cost_estimate=cost(30 * shares),
        name="relations",
    )(length, split, block, teacher, own, packed, small)


def norm_forward(rows, gain, shift):
    center = jnp.mean(rows, axis=1, keepdims=True)
    offsets = rows - center
    rstd = lax.rsqrt(jnp.mean(offsets * offsets, axis=1, keepdims=True) + NORM_EPS)
    normed = offsets * rstd
    return normed * gain + shift, normed, rstd


def norm_backward(grad, normed, rstd, gain):
    inner = grad * gain
    mean = jnp.mean(inner, axis=1, keepdims=True)
    slope = jnp.mean(inner * normed, axis=1, keepdims=True)
    return rstd * (inner - mean - normed * slope)


def gelu_terms(x):
    size = jnp.abs(x) * math.sqrt(0.5)
    t = 1.0 / (1.0 + 0.3275911 * size)
    bell = jnp.exp(-0.5 * x * x)
    poly = t * (0.254829592 + t * (-0.284496736 + t * (1.421413741 + t * (-1.453152027 + t * 1.061405429))))
    tail = 0.5 * poly * bell
    share = jnp.where(x >= 0.0, 1.0 - tail, tail)
    return x * share, share + x * bell * (1.0 / math.sqrt(2.0 * math.pi))


def unpack_all(own_ref, packed_ref, pack):
    pack[0] = own_ref[...]
    for share in range(1, pack.shape[0]):
        unpack(packed_ref, share - 1, pack.at[share])


def mid_part(packed):
    return whole(packed.shape[:2] + (part_rows(MID_ROWS, packed.shape[0]), packed.shape[3]))


def split_pack(pack):
    return pack.at[:, :D], pack.at[:, D : 2 * D], pack.at[:, 2 * D :]


def block_kernel(
    length_ref, x_ref, own_ref, packed_ref, small_ref, branch_ref, gain_ref, shift_ref, first_ref, other_ref,
    block_ref, n1_ref, r1_ref, n2_ref, r2_ref, act_ref, slope_ref, sums_ref, pack,
):
    shares = small_ref.shape[0]
    a_refs = [first_ref.at[0]] + [other_ref.at[s] for s in range(shares - 1)]
    tile = x_ref.shape[0]

    @pl.when(pl.program_id(0) == 0)
    def _():
        unpack_all(own_ref, packed_ref, pack)

    wide_ref, narrow_ref, out_ref = split_pack(pack)
    x = x_ref[...].astype(f32)
    mixing = branch_ref[0:1, :]
    for s in range(shares):
        mixing = mixing + dot(a_refs[s][:, :96], out_ref[s, :96, :])
    middle, normed, rstd = norm_forward(x + mixing, gain_ref[0:1, :], shift_ref[0:1, :])
    n1_ref[...] = normed
    r1_ref[...] = rstd
    low = middle.astype(bf16)
    branch = branch_ref[1:2, :]
    width = D
    for s in range(shares):
        value, slope = gelu_terms(dot(low, wide_ref[s]) + small_ref[s, 4:5, :].astype(f32))
        value = value.astype(bf16)
        act_ref[:, s * width : (s + 1) * width] = value
        slope_ref[:, s * width : (s + 1) * width] = slope.astype(bf16)
        branch = branch + dot(value, narrow_ref[s])
    block, normed, rstd = norm_forward(middle + branch, gain_ref[1:2, :], shift_ref[1:2, :])
    n2_ref[...] = normed
    r2_ref[...] = rstd
    block_ref[...] = block.astype(bf16)
    position = lax.broadcasted_iota(jnp.int32, (tile, 1), 0) + pl.program_id(0) * tile
    kept = jnp.where(position < own_number(length_ref), 1.0, 0.0)
    row = lax.broadcasted_iota(jnp.int32, (8, x.shape[1]), 0)
    total = jnp.zeros((8, x.shape[1]), f32)
    for index, part in enumerate((x, mixing, branch)):
        total = jnp.where(row == index, jnp.sum(kept * part * part, axis=0, keepdims=True), total)

    @pl.when(pl.program_id(0) == 0)
    def _():
        sums_ref[...] = jnp.zeros_like(sums_ref)

    sums_ref[...] += total


def by_tile(tile, width):
    return pl.BlockSpec((tile, width), lambda i: (i, 0))


def block_forward(length, x, attended, own, packed, small, branch_bias, gain, shift):
    rows, width = x.shape
    tile = min(256, rows)
    shares = small.shape[0]
    units = shares * D
    row, column = by_tile(tile, width), by_tile(tile, 1)
    return pl.pallas_call(
        block_kernel,
        grid=(rows // tile,),
        in_specs=[
            SMEM, row, whole(own.shape), mid_part(packed), whole(small.shape), whole(branch_bias.shape), whole(gain.shape), whole(shift.shape),
        ] + [pl.BlockSpec((a.shape[0], tile, 128), lambda i: (0, i, 0)) for a in attended],
        out_specs=[row, row, column, row, column, by_tile(tile, units), by_tile(tile, units), whole((8, width))],
        out_shape=[
            jax.ShapeDtypeStruct((rows, width), bf16),
            jax.ShapeDtypeStruct((rows, width), f32),
            jax.ShapeDtypeStruct((rows, 1), f32),
            jax.ShapeDtypeStruct((rows, width), f32),
            jax.ShapeDtypeStruct((rows, 1), f32),
            jax.ShapeDtypeStruct((rows, units), bf16),
            jax.ShapeDtypeStruct((rows, units), bf16),
            jax.ShapeDtypeStruct((8, width), f32),
        ],
        scratch_shapes=[pltpu.VMEM((shares, 2 * D + 128, D), bf16)],
        compiler_params=pltpu.CompilerParams(vmem_limit_bytes=VMEM),
        cost_estimate=cost(20),
        name="block_forward",
    )(length, x, own, packed, small, branch_bias, gain, shift, *attended)


def block_backward_kernel(
    length_ref, d_ref, n1_ref, r1_ref, n2_ref, r2_ref, act_ref, slope_ref, own_ref, packed_ref, gain_ref,
    shift_ref, kl_ref, square_ref, six_ref, first_ref, other_ref, *rest,
):
    step = pl.program_id(0)
    pack = rest[-1]
    shares = pack.shape[0]
    a_refs = [first_ref.at[0]] + [other_ref.at[s] for s in range(shares - 1)]
    sum_ref, da_refs = rest[0], rest[1 : shares + 1]
    g_ref, tail_ref, vec_ref, g_sum, low_s, branch_s, pre_s, mix_s = rest[shares + 1 : -1]
    tile, width = d_ref.shape
    units = D
    span = pl.ds(pl.multiple_of(step * tile, tile), tile)

    @pl.when(step == 0)
    def _():
        unpack_all(own_ref, packed_ref, pack)
        vec_ref[...] = jnp.zeros_like(vec_ref)
        g_sum[...] = jnp.zeros_like(g_sum)

    wide_ref, narrow_ref, out_ref = split_pack(pack)

    def column(value):
        return jnp.sum(value, axis=0, keepdims=True)

    row = lax.broadcasted_iota(jnp.int32, (8, width), 0)
    d_block = d_ref[...]
    normed_two = n2_ref[...]
    d_two = norm_backward(d_block, normed_two, r2_ref[...], gain_ref[1:2, :])
    d_branch = d_two.astype(bf16)
    branch_s[span, :] = d_branch
    normed_one = n1_ref[...]
    low = (normed_one * gain_ref[0:1, :] + shift_ref[0:1, :]).astype(bf16)
    low_s[span, :] = low
    d_middle = d_two
    for s in range(shares):
        grad = dot(d_branch, narrow_ref[s], NT) * slope_ref[:, s * units : (s + 1) * units].astype(f32)
        grad = grad.astype(bf16)
        pre_s[span, s * units : (s + 1) * units] = grad
        g_sum[s : s + 1, :] += column(grad.astype(f32))
        d_middle = d_middle + dot(grad, wide_ref[s], NT)
    d_one = norm_backward(d_middle, normed_one, r1_ref[...], gain_ref[0:1, :])
    sum_ref[...] = d_one
    d_mixing = d_one.astype(bf16)
    mix_s[span, :] = d_mixing
    for s in range(shares):
        da_refs[s][...] = wide_rows(dot(d_mixing, out_ref[s, :96, :], NT)).astype(bf16)
    parts = (
        d_mixing.astype(f32), d_branch.astype(f32), d_middle * normed_one, d_block * normed_two, d_middle, d_block,
    )
    total = jnp.zeros((8, width), f32)
    for index, part in enumerate(parts):
        total = jnp.where(row == index, column(part), total)
    vec_ref[...] += total

    @pl.when(step == pl.num_programs(0) - 1)
    def _():
        for s in range(shares):
            part = slice(s * units, (s + 1) * units)
            own = slice(s * width, (s + 1) * width)
            g_ref[0:units, own] = dot(act_ref[:, part], branch_s[...], TN).astype(bf16)
            g_ref[units : 2 * units, own] = dot(low_s[...], pre_s[:, part], TN).astype(bf16)
            g_ref[2 * units : 2 * units + 96, own] = dot(a_refs[s][...], mix_s[...], TN)[:96].astype(bf16)
            g_ref[2 * units + 128 :, own] = six_ref[s]
            first = lax.broadcasted_iota(jnp.int32, (32, units), 0) == 0
            g_ref[2 * units + 96 : 2 * units + 128, own] = jnp.where(first, g_sum[s : s + 1, :], 0.0).astype(bf16)
        scalars = [jnp.sum(kl_ref[...], axis=0, keepdims=True)]
        scalars += [jnp.sum(square_ref[i : i + 1, :], axis=1, keepdims=True) for i in range(3)]
        scalars += [jnp.broadcast_to(own_number(length_ref).astype(f32), (1, 1))]
        lane = lanes((8, width))
        total = vec_ref[...]
        for index, value in enumerate(scalars):
            total = jnp.where((row == 6) & (lane == index), value, total)
        total = jnp.concatenate([jnp.zeros((2, width), f32), total, jnp.zeros((6, width), f32)], axis=0)
        high = total.astype(bf16).astype(f32)
        tail_ref[:16, :] = high.astype(bf16)
        tail_ref[16:, :] = (total - high).astype(bf16)


def block_backward(
    length, d_block, n1, r1, n2, r2, act, slope, attended, own, packed, gain, shift, divergence, squares, six,
):
    rows, width = d_block.shape
    tile = min(256, rows)
    shares, units = six.shape[0], D
    row, column = by_tile(tile, width), by_tile(tile, 1)
    return pl.pallas_call(
        block_backward_kernel,
        grid=(rows // tile,),
        in_specs=[
            SMEM, row, row, column, row, column, whole(act.shape), by_tile(tile, shares * units), whole(own.shape), mid_part(packed), whole(gain.shape), whole(shift.shape),
            whole(divergence.shape), whole(squares.shape), whole(six.shape),
        ] + [whole(a.shape) for a in attended],
        out_specs=[
            row, *[by_tile(tile, 128)] * shares, whole((2 * units + 448, shares * width)), whole((32, width)),
        ],
        out_shape=[
            jax.ShapeDtypeStruct((rows, width), f32),
            *[jax.ShapeDtypeStruct((rows, 128), bf16)] * shares,
            jax.ShapeDtypeStruct((2 * units + 448, shares * width), bf16),
            jax.ShapeDtypeStruct((32, width), bf16),
        ],
        scratch_shapes=[
            pltpu.VMEM((8, width), f32),
            pltpu.VMEM((8, units), f32),
            pltpu.VMEM((rows, width), bf16),
            pltpu.VMEM((rows, width), bf16),
            pltpu.VMEM((rows, shares * units), bf16),
            pltpu.VMEM((rows, width), bf16),
            pltpu.VMEM((shares, 2 * D + 128, D), bf16),
        ],
        compiler_params=pltpu.CompilerParams(vmem_limit_bytes=VMEM),
        cost_estimate=cost(25),
        name="block_backward",
    )(
        length, d_block, n1, r1, n2, r2, act, slope, own, packed, gain, shift, divergence, squares, six, *attended
    )


def after(value, *others):
    return lax.optimization_barrier((value,) + others)[0]


def shift_shares(value, by):
    shares = lax.axis_size("heads")
    return lax.ppermute(value, "heads", [((i + by) % shares, i) for i in range(shares)])


def exchange(value, bit):
    size = lax.axis_size("batch")
    return lax.ppermute(value, "batch", [(i, i ^ bit) for i in range(size)])


def merge_kernel(*refs, count):
    outs = refs[count:]
    total = refs[0][...].astype(f32)
    for ref in refs[1:count]:
        total = total + ref[...].astype(f32)
    end = total.shape[0] - 32
    sums = total[end : end + 16] + total[end + 16 :]
    if len(outs) == 2:
        put_turned(total[:end], outs[0])
        outs[1][...] = sums
    else:
        high = sums.astype(bf16).astype(f32)
        outs[0][:end, :] = total[:end].astype(bf16)
        outs[0][end : end + 16, :] = high.astype(bf16)
        outs[0][end + 16 :, :] = (sums - high).astype(bf16)


def put_turned(rows, out_ref):
    for part in range(3):
        out_ref[:, part, :] = rows[part * 96 : (part + 1) * 96].T


def merge(parts, last=False):
    rows, width = parts[0].shape
    if last:
        shape = [jax.ShapeDtypeStruct((width, 3, 96), f32), jax.ShapeDtypeStruct((16, width), f32)]
    else:
        shape = jax.ShapeDtypeStruct((rows, width), bf16)
    return pl.pallas_call(
        functools.partial(merge_kernel, count=len(parts)), out_shape=shape, cost_estimate=cost(1), name="merge",
        compiler_params=pltpu.CompilerParams(vmem_limit_bytes=VMEM),
    )(*parts)


def finish_mid_kernel(rows_ref, narrow_ref, wide_ref, out_ref, bias_ref, six_ref, sums_ref):
    units = narrow_ref.shape[0]
    narrow_ref[...] = rows_ref[:units, :].astype(f32)
    wide_ref[...] = rows_ref[units : 2 * units, :].astype(f32)
    out_ref[...] = rows_ref[2 * units : 2 * units + 96, :].astype(f32)
    bias_ref[...] = rows_ref[2 * units + 96 : 2 * units + 112, :].astype(f32)[:8]
    six = 2 * units + 128
    put_turned(rows_ref[six : six + 288, :].astype(f32), six_ref)
    sums_ref[...] = rows_ref[six + 288 : six + 304, :].astype(f32) + rows_ref[six + 304 :, :].astype(f32)


def finish_mid(rows):
    width = rows.shape[1]
    shapes = [(D, width), (D, width), (96, width), (8, width), (width, 3, 96), (16, width)]
    return pl.pallas_call(
        finish_mid_kernel, out_shape=[jax.ShapeDtypeStruct(s, f32) for s in shapes], cost_estimate=cost(1),
        name="finish_mid", compiler_params=pltpu.CompilerParams(vmem_limit_bytes=VMEM),
    )(rows)


def body(
    student_rows, teacher_rows, valid_length, split_point, project_five, bias_five, output_five, branch_bias,
    norm_gain, norm_bias, widen_weight, widen_bias, narrow_weight, project_six, bias_six, teacher_project,
    teacher_bias,
):
    shares = lax.axis_size("heads")
    batch = lax.axis_size("batch")
    place = lax.axis_index("batch")
    all_rows = shares * batch * HEADS
    x = student_rows[0]
    teacher = teacher_rows[0]

    def turned(weight):
        return jnp.transpose(weight, (1, 2, 0)).reshape(-1, weight.shape[0])

    def pad(rows, width):
        return jnp.pad(rows, ((0, 0), (0, width - rows.shape[1])))

    small = jnp.concatenate(
        [pad(bias_five, D), pad(bias_six, D), widen_bias[None], pad(teacher_bias, D), jnp.zeros((9, D), bf16)], axis=0
    )
    five = jnp.concatenate([turned(project_five), small], axis=0)

    def part_of(rows):
        count = part_rows(rows.shape[0], batch)
        rows = jnp.pad(rows, ((0, count * batch - rows.shape[0]), (0, 0)))
        return lax.dynamic_slice_in_dim(rows, place * count, count)

    def others(rows):
        return [shift_shares(rows, by) for by in range(1, shares)]

    half = five.shape[0] // 2
    core = lax.rem(place, 2)
    halves = others(lax.dynamic_slice_in_dim(five, core * half, half))
    mid = jnp.concatenate([widen_weight, narrow_weight, jnp.pad(output_five, ((0, 32), (0, 0)))], axis=0)
    taught = turned(teacher_project)
    rest = jnp.concatenate([turned(project_six), taught[:, :D], taught[:, D:]], axis=0)
    parts = others(after(jnp.concatenate([part_of(mid), part_of(rest)], axis=0), five))

    first = attend_forward(valid_length, x, five[None])
    halves = jnp.stack([after(p, first[5]) for p in halves])
    swapped = exchange(halves, 1)
    parts = jnp.stack([after(p, first[5], halves) for p in parts])
    parts_all = lax.all_gather(parts, "batch", axis=0)
    low, high = jnp.where(core == 0, halves, swapped), jnp.where(core == 0, swapped, halves)
    fives = jnp.concatenate([low, high], axis=1)
    smalls = jnp.concatenate([five[None, 288:], fives[:, 288:]], axis=0)
    other = attend_forward(valid_length, after(x, parts), fives)
    attended = (first[5], other[5])
    block, n1, r1, n2, r2, act, slope, squares = block_forward(
        valid_length, x, attended, mid, parts_all, smalls, branch_bias, norm_gain, norm_bias
    )
    d_block, g_six, divergence = relations(
        valid_length, split_point, block, teacher, rest, parts_all, smalls, all_rows
    )
    result = block_backward(
        valid_length, d_block, n1, r1, n2, r2, act, slope, attended, mid, parts_all, norm_gain, norm_bias,
        divergence, squares, g_six,
    )
    d_sum_one, d_attended, (g_both, tail) = result[0], result[1 : 1 + shares], result[1 + shares :]

    def to_owner(parts):
        return [parts[0]] + [shift_shares(parts[by], shares - by) for by in range(1, shares)]

    units = widen_weight.shape[1]
    both = lax.psum_scatter(g_both, "batch", scatter_dimension=0, tiled=True)

    grad_in = d_sum_one
    g_five = [None] * shares
    for s in list(range(1, shares)) + [0]:
        q, k, v, e, r, a = other if s else first
        rows, w = after(x, *g_five[1 : shares - 1]) if s == 0 else x, fives if s else five[None]
        grad, grad_in = attend_backward(max(s - 1, 0), q, k, v, e, r, a, d_attended[s], rows, w, grad_in, tail)
        g_five[s] = shift_shares(grad, shares - s) if s else grad

    five_sum = merge(g_five)
    both = after(both, five_sum)
    both = to_owner([both[:, s * D : (s + 1) * D] for s in range(shares)])
    bit = 1
    while 2 * bit < batch:
        five_sum = merge([five_sum, exchange(five_sum, bit)])
        if bit == 1:
            both = [after(p, five_sum) for p in both]
        bit *= 2
    both = sum(p.astype(f32) for p in both).astype(bf16)
    both = lax.all_gather(both, "batch", axis=0, tiled=True)
    grad_five, five_sums = merge([five_sum, exchange(five_sum, bit)], last=True)
    grad_narrow, grad_wide, grad_out, wide_bias, grad_six, six_sums = finish_mid(both)
    totals = five_sums[8]
    counted = totals[4] * D
    summary = jnp.concatenate([totals[:1], jnp.sqrt(totals[1:4] / counted)])
    return (
        block[None], grad_in[None], grad_five, five_sums[0:2, :96],
        grad_out, five_sums[2:4], five_sums[4:6], five_sums[6:8],
        grad_wide, wide_bias[0], grad_narrow, grad_six, six_sums[0:2, :96], summary,
    )


def solution(mesh):
    return jax.shard_map(
        body,
        mesh=mesh,
        in_specs=(
            P(("batch", "heads"), None, None),
            P(("batch", "heads"), None, None),
            P("batch"),
            P("batch"),
            P(None, None, "heads"),
            P(None, "heads"),
            P("heads", None),
            P(),
            P(),
            P(),
            P(None, "heads"),
            P("heads"),
            P("heads", None),
            P(None, None, "heads"),
            P(None, "heads"),
            P(None, None, "heads"),
            P(None, "heads"),
        ),
        out_specs=(
            P(("batch", "heads"), None, None),
            P(("batch", "heads"), None, None),
            P(None, None, "heads"),
            P(None, "heads"),
            P("heads", None),
            P(),
            P(),
            P(),
            P(None, "heads"),
            P("heads"),
            P("heads", None),
            P(None, None, "heads"),
            P(None, "heads"),
            P(),
        ),
        check_vma=False,
    )
```

profile of v0, /device:TPU:0, one launch (start us, length us, event | category | flops | bytes accessed | tf_op | source)
XLA Modules:
  0.0 422.2 jit_solution(11695448532563814094)
XLA Ops:
  7.3 0.7 broadcast_in_dim.19
  8.0 0.7 pad.21
  8.7 0.7 pad.22
  9.3 0.7 pad.23
  10.0 1.2 concatenate.28
  11.2 3.1 collective-permute-start.3
  14.3 2.6 collective-permute-start.2
  16.9 1.3 collective-permute-start.1
  18.3 1.3 fusion.2
  19.6 0.1 fusion.1.own_ref
  19.7 0.1 pad_maximum_fusion.own_ref
  19.9 0.6 copy-done
  20.5 0.7 collective-permute-start.5
  21.3 0.3 collective-permute-start.4
  21.6 2.8 collective-permute-start
  24.4 9.3 %attend_forward.2 = (bf16[1,1024,128]{2,1,0:T(8,128)(2,1)}, bf16[1,1024,128]{2,1,0:T(8,128)(2,1)}, bf16[1,1024,128]{2,1,0:T(8,128)(2,1)}, bf16[1,3,1024,1024]{3,...) custom-call(s32[4]{0:T(128)} %length_ref.9, bf16[1024,384]{1,0:T(8,128)(2,1)} %bitcast.29, ...), custom_call_target="tpu_custom_call" | custom-call | flops 360000000 | bytes 1024 | tf_op jit(solution)/shard_map/attend_forward/pallas_call | solution.py:225
  33.8 8.3 %collective-permute-done.4 = bf16[304,384]{1,0:T(8,128)(2,1)S(1)} collective-permute-done((bf16[304,384]{1,0:T(8,128)(2,1)S(1)}, bf16[304,384]{1,0:T(8,128)(2,1)S(1)}, u32[]{:S(2)}, u32[]{:S(2)}) %collective-permute-start.4) | collective-permute-done | bytes 233504 | tf_op jit(solution)/shard_map/ppermute | solution.py:949
  42.1 0.9 pad_maximum_fusion.1
  43.1 0.3 reduce-scatter.2.cloned.1.call-start
  43.4 0.1 collective-permute-start.6
  43.5 0.2 concatenate.29
  43.7 1.4 collective-permute-done.6
  45.2 0.1 broadcast_select_fusion
  45.3 0.9 pad_maximum_fusion.2.w_ref.w_hbm
  46.2 23.0 %attend_forward.3 = (bf16[3,1024,128]{2,1,0:T(8,128)(2,1)}, bf16[3,1024,128]{2,1,0:T(8,128)(2,1)}, bf16[3,1024,128]{2,1,0:T(8,128)(2,1)}, bf16[3,3,1024,1024]{3,...) custom-call(s32[4]{0:T(128)} %length_ref.9, bf16[1024,384]{1,0:T(8,128)(2,1)} %bitcast.30, ...), custom_call_target="tpu_custom_call" | custom-call | flops 1080000000 | bytes 1024 | tf_op jit(solution)/shard_map/attend_forward/pallas_call | solution.py:225
  69.2 0.6 pad_maximum_fusion.5.small_ref
  69.8 20.3 %all-gather.3.cloned.1.call-done = bf16[24,304,384]{2,1,0:T(8,128)(2,1)} async-done(((bf16[3,304,384]{2,1,0:T(8,128)(2,1)}), bf16[24,304,384]{2,1,0:T(8,128)(2,1)}) %all-gather.3.cloned.1.call-update) | async-done | bytes 5603344 | tf_op jit(solution)/shard_map/all_gather | solution.py:1054
  90.1 17.1 %block_forward.1 = (bf16[1024,384]{1,0:T(8,128)(2,1)}, f32[1024,384]{1,0:T(8,128)}, f32[1024,1]{1,0:T(8,128)}, f32[1024,384]{1,0:T(8,128)}, f32[1024,1]{1,0:T(8,...) custom-call(s32[4]{0:T(128)} %length_ref.9, bf16[1024,384]{1,0:T(8,128)(2,1)} %bitcast.31, ...), custom_call_target="tpu_custom_call" | custom-call | flops 800000000 | bytes 1024 | tf_op jit(solution)/shard_map/block_forward/pallas_call | solution.py:800
  107.2 129.7 %relations.1 = (f32[1024,384]{1,0:T(8,128)}, bf16[4,320,384]{2,1,0:T(8,128)(2,1)}, f32[1024,1]{1,0:T(8,128)}) custom-call(s32[4]{0:T(128)} %length_ref.9, s32[4]{0:T(128)} %split_ref.1, bf16[1024,384]{1,0:T(8,128)(2,1)} %get-tuple-element.84.block_ref, bf16[1024,768]{1,0:T(8,128)(2,1)} %bitcast.51, bf16[1440,384]{1,0:T(8,128)(2,1)} %copy-done.1, ...), custom_call_target="tpu_custom_call" | custom-call | flops 4800000000 | bytes 1024 | tf_op jit(solution)/shard_map/relations/pallas_call | solution.py:668
  236.9 19.7 %block_backward.1 = (f32[1024,384]{1,0:T(8,128)}, bf16[1024,128]{1,0:T(8,128)(2,1)}, bf16[1024,128]{1,0:T(8,128)(2,1)}, bf16[1024,128]{1,0:T(8,128)(2,1)}, bf16[...) custom-call(s32[4]{0:T(128)} %length_ref.9, f32[1024,384]{1,0:T(8,128)} %get-tuple-element.90.d_ref, ...), custom_call_target="tpu_custom_call" | custom-call | flops 1000000000 | bytes 1024 | tf_op jit(solution)/shard_map/block_backward/pallas_call | solution.py:910
  256.7 11.6 %attend_backward.4 = (bf16[320,384]{1,0:T(8,128)(2,1)}, f32[1024,384]{1,0:T(8,128)}) custom-call(bf16[3,1024,128]{2,1,0:T(8,128)(2,1)} %get-tuple-element.101.q_ref, bf16[3,1024,128]{2,1,0:T(8,128)(2,1)} %get-tuple-element.102.k_ref, bf16[3,1024,128]{2,1,0:T(8,128)(2,1)} %get-tuple-element.103.v_ref, bf16[3,3,1024,1024]{3,2,1,0:T(8,128)(2,1)} %get-tuple-element.104.e_hbm, ...), custom_call_target="tpu_custom_call" | custom-call | flops 400000000 | bytes 1024 | tf_op jit(solution)/shard_map/attend_backward/pallas_call | solution.py:369
  268.3 5.6 %collective-permute-start.7 = (bf16[320,384]{1,0:T(8,128)(2,1)}, bf16[320,384]{1,0:T(8,128)(2,1)S(1)}, u32[]{:S(2)}, u32[]{:S(2)}) collective-permute-start(bf16[320,384]{1,0:T(8,128)(2,1)} %get-tuple-element.109), channel_id=1, source_target_pairs={{24,0},{0,8},{8,16},{16,24},{25,1},{1,9},{9,17},{17,25},{26,2},{2,... | collective-permute-start | bytes 737288 | tf_op jit(solution)/shard_map/ppermute | solution.py:949
  273.9 11.8 %attend_backward.5 = (bf16[320,384]{1,0:T(8,128)(2,1)}, f32[1024,384]{1,0:T(8,128)}) custom-call(bf16[3,1024,128]{2,1,0:T(8,128)(2,1)} %get-tuple-element.101.q_ref, bf16[3,1024,128]{2,1,0:T(8,128)(2,1)} %get-tuple-element.102.k_ref, bf16[3,1024,128]{2,1,0:T(8,128)(2,1)} %get-tuple-element.103.v_ref, bf16[3,3,1024,1024]{3,2,1,0:T(8,128)(2,1)} %get-tuple-element.104.e_hbm, ...), custom_call_target="tpu_custom_call" | custom-call | flops 400000000 | bytes 1024 | tf_op jit(solution)/shard_map/attend_backward/pallas_call | solution.py:369
  285.7 2.4 collective-permute-start.8
  288.1 11.6 %attend_backward.6 = (bf16[320,384]{1,0:T(8,128)(2,1)}, f32[1024,384]{1,0:T(8,128)}) custom-call(bf16[3,1024,128]{2,1,0:T(8,128)(2,1)} %get-tuple-element.101.q_ref, bf16[3,1024,128]{2,1,0:T(8,128)(2,1)} %get-tuple-element.102.k_ref, bf16[3,1024,128]{2,1,0:T(8,128)(2,1)} %get-tuple-element.103.v_ref, bf16[3,3,1024,1024]{3,2,1,0:T(8,128)(2,1)} %get-tuple-element.104.e_hbm, ...), custom_call_target="tpu_custom_call" | custom-call | flops 400000000 | bytes 1024 | tf_op jit(solution)/shard_map/attend_backward/pallas_call | solution.py:369
  299.7 0.1 collective-permute-start.9
  299.8 12.0 %attend_backward.7 = (bf16[320,384]{1,0:T(8,128)(2,1)}, f32[1024,384]{1,0:T(8,128)}) custom-call(bf16[1,1024,128]{2,1,0:T(8,128)(2,1)} %get-tuple-element.85.q_ref, bf16[1,1024,128]{2,1,0:T(8,128)(2,1)} %get-tuple-element.86.k_ref, bf16[1,1024,128]{2,1,0:T(8,128)(2,1)} %get-tuple-element.87.v_ref, bf16[1,3,1024,1024]{3,2,1,0:T(8,128)(2,1)} %get-tuple-element.88.e_hbm, ...), custom_call_target="tpu_custom_call" | custom-call | flops 400000000 | bytes 1024 | tf_op jit(solution)/shard_map/attend_backward/pallas_call | solution.py:369
  311.9 0.7 copy-done.7
  312.6 2.1 merge.4.refs_0_
  314.7 40.2 %collective-permute-start.10 = (bf16[320,384]{1,0:T(8,128)(2,1)}, bf16[320,384]{1,0:T(8,128)(2,1)S(1)}, u32[]{:S(2)}, u32[]{:S(2)}) collective-permute-start(bf16[320,384]{1,0:T(8,128)(2,1)} %merge.4.refs_0_), channel_id=1, source_target_pairs={{0,1},{1,0},{2,3},{3,2},{4,5},{5,4},{6,7},{7,6},{8,9},{9,8},{10,11... | collective-permute-start | bytes 737288 | tf_op jit(solution)/shard_map/ppermute | solution.py:954
  354.9 1.3 collective-permute-done.10.refs_1_
  356.2 0.7 copy-done.9
  356.9 1.8 merge.5.refs_0_
  358.7 8.4 %collective-permute-done.11.refs_1_ = bf16[320,384]{1,0:T(8,128)(2,1)S(1)} collective-permute-done((bf16[320,384]{1,0:T(8,128)(2,1)}, bf16[320,384]{1,0:T(8,128)(2,1)S(1)}, u32[]{:S(2)}, u32[]{:S(2)}) %collective-permute-start.11) | collective-permute-done | bytes 245792 | tf_op jit(solution)/shard_map/ppermute | solution.py:954
  367.2 0.7 copy-done.10
  367.9 1.8 merge.6.refs_0_
  369.7 7.6 %collective-permute-done.12.refs_1_ = bf16[320,384]{1,0:T(8,128)(2,1)S(1)} collective-permute-done((bf16[320,384]{1,0:T(8,128)(2,1)}, bf16[320,384]{1,0:T(8,128)(2,1)S(1)}, u32[]{:S(2)}, u32[]{:S(2)}) %collective-permute-start.12) | collective-permute-done | bytes 245792 | tf_op jit(solution)/shard_map/ppermute | solution.py:954
  377.3 0.7 copy-done.8
  378.0 2.4 merge.7
  380.4 1.3 fusion.4
  382.4 1.4 fusion.5
  383.8 1.1 fusion.3
  384.9 1.8 collective-permute-start.15
  386.7 0.8 collective-permute-start.13
  387.5 0.8 sqrt_bitcast_fusion
  388.3 1.3 slice.60
  389.5 2.1 copy.33
  391.7 1.2 pad_maximum_fusion.6
  392.9 3.4 collective-permute-done.14
  396.4 10.8 %all_gather.11.rows_ref = bf16[1216,384]{1,0:T(8,128)(2,1)} all-gather(bf16[152,384]{1,0:T(8,128)(2,1)S(1)} %add_convert_fusion), channel_id=1, replica_groups=mesh['heads'=4,'batch'=8] {'batch'}, dimensions={0}, use_global_device_ids=true | all-gather | bytes 1050624 | tf_op jit(solution)/shard_map/all_gather | solution.py:1096
  407.2 2.9 finish_mid.1
  410.2 1.2 slice.69
  411.4 1.3 slice_reduce_fusion
  412.7 2.1 copy.34
  (46 shorter events, 0.4 us)
Async XLA Ops:
  7.2 12.4 %copy-start.3 = (bf16[384,384]{1,0:T(8,128)(2,1)S(1)}, bf16[384,384]{1,0:T(8,128)(2,1)}, u32[]{:S(2)}) copy-start(bf16[384,384]{1,0:T(8,128)(2,1)} %param.29) | copy-start | bytes 884740
  7.2 12.4 %copy-start.4 = (bf16[384,384]{1,0:T(8,128)(2,1)S(1)}, bf16[384,384]{1,0:T(8,128)(2,1)}, u32[]{:S(2)}) copy-start(bf16[384,384]{1,0:T(8,128)(2,1)} %param.27) | copy-start | bytes 884740
  7.2 12.4 %copy-start.12 = (bf16[96,384]{1,0:T(8,128)(2,1)S(1)}, bf16[96,384]{1,0:T(8,128)(2,1)}, u32[]{:S(2)}) copy-start(bf16[96,384]{1,0:T(8,128)(2,1)} %param.23) | copy-start | bytes 221188
  7.2 82.9 %all-gather.3.cloned.1.call-start = ((), (), s32[]{:S(2)}) async-start(), calls=%async_computation.2 | async-start | bytes 6303744 | tf_op jit(solution)/shard_map/all_gather | solution.py:1054
  11.2 8.4 %copy-start.2 = (bf16[304,384]{1,0:T(8,128)(2,1)}, bf16[304,384]{1,0:T(8,128)(2,1)S(1)}, u32[]{:S(2)}) copy-start(bf16[304,384]{1,0:T(8,128)(2,1)S(1)} %concatenate.28) | copy-start | bytes 700420
  11.2 10.4 %collective-permute-start.3 = (bf16[152,384]{1,0:T(8,128)(2,1)S(1)}, bf16[152,384]{1,0:T(8,128)(2,1)S(1)}, u32[]{:S(2)}, u32[]{:S(2)}) collective-permute-start(bf16[152,384]{1,0:T(8,128)(2,1)S(1)} %constant_dynamic-slice_fusion), channel_id=1, source_target_pairs={{24,0},{0,8},{8,16},{16,24},{25,1},{1,9},{9,17},{17,25},{26,2},{2,... | collective-permute-start | bytes 350216 | tf_op jit(solution)/shard_map/ppermute | solution.py:949
  14.3 19.4 %collective-permute-start.2 = (bf16[152,384]{1,0:T(8,128)(2,1)S(1)}, bf16[152,384]{1,0:T(8,128)(2,1)S(1)}, u32[]{:S(2)}, u32[]{:S(2)}) collective-permute-start(bf16[152,384]{1,0:T(8,128)(2,1)S(1)} %constant_dynamic-slice_fusion), channel_id=1, source_target_pairs={{16,0},{24,8},{0,16},{8,24},{17,1},{25,9},{1,17},{9,25},{18,2},{26... | collective-permute-start | bytes 350216 | tf_op jit(solution)/shard_map/ppermute | solution.py:949
  16.9 16.8 %collective-permute-start.1 = (bf16[152,384]{1,0:T(8,128)(2,1)S(1)}, bf16[152,384]{1,0:T(8,128)(2,1)S(1)}, u32[]{:S(2)}, u32[]{:S(2)}) collective-permute-start(bf16[152,384]{1,0:T(8,128)(2,1)S(1)} %constant_dynamic-slice_fusion), channel_id=1, source_target_pairs={{8,0},{16,8},{24,16},{0,24},{9,1},{17,9},{25,17},{1,25},{10,2},{18... | collective-permute-start | bytes 350216 | tf_op jit(solution)/shard_map/ppermute | solution.py:949
  18.3 1.4 copy-start.11
  19.7 0.9 copy-start
  19.8 14.0 %copy-start.1 = (bf16[1440,384]{1,0:T(8,128)(2,1)}, bf16[1440,384]{1,0:T(8,128)(2,1)S(1)}, u32[]{:S(2)}) copy-start(bf16[1440,384]{1,0:T(8,128)(2,1)S(1)} %pad_maximum_fusion.own_ref) | copy-start | bytes 3317764
  20.5 13.3 %collective-permute-start.5 = (bf16[304,384]{1,0:T(8,128)(2,1)S(1)}, bf16[304,384]{1,0:T(8,128)(2,1)S(1)}, u32[]{:S(2)}, u32[]{:S(2)}) collective-permute-start(bf16[304,384]{1,0:T(8,128)(2,1)S(1)} %pad_maximum_fusion.4), channel_id=1, source_target_pairs={{24,0},{0,8},{8,16},{16,24},{25,1},{1,9},{9,17},{17,25},{26,2},{2,... | collective-permute-start | bytes 700424 | tf_op jit(solution)/shard_map/ppermute | solution.py:949
  21.3 20.9 %collective-permute-start.4 = (bf16[304,384]{1,0:T(8,128)(2,1)S(1)}, bf16[304,384]{1,0:T(8,128)(2,1)S(1)}, u32[]{:S(2)}, u32[]{:S(2)}) collective-permute-start(bf16[304,384]{1,0:T(8,128)(2,1)S(1)} %pad_maximum_fusion.4), channel_id=1, source_target_pairs={{16,0},{24,8},{0,16},{8,24},{17,1},{25,9},{1,17},{9,25},{18,2},{26... | collective-permute-start | bytes 700424 | tf_op jit(solution)/shard_map/ppermute | solution.py:949
  21.6 20.5 %collective-permute-start = (bf16[304,384]{1,0:T(8,128)(2,1)S(1)}, bf16[304,384]{1,0:T(8,128)(2,1)S(1)}, u32[]{:S(2)}, u32[]{:S(2)}) collective-permute-start(bf16[304,384]{1,0:T(8,128)(2,1)S(1)} %pad_maximum_fusion.4), channel_id=1, source_target_pairs={{8,0},{16,8},{24,16},{0,24},{9,1},{17,9},{25,17},{1,25},{10,2},{18... | collective-permute-start | bytes 700424 | tf_op jit(solution)/shard_map/ppermute | solution.py:949
  43.1 340.7 %reduce-scatter.2.cloned.1.call-start = ((), (), s32[]{:S(2)}) async-start(), calls=%async_computation.1 | async-start | bytes 4202496 | tf_op jit(solution)/shard_map/reduce_scatter | solution.py:1076
  43.4 1.7 collective-permute-start.6
  268.3 31.5 %collective-permute-start.7 = (bf16[320,384]{1,0:T(8,128)(2,1)}, bf16[320,384]{1,0:T(8,128)(2,1)S(1)}, u32[]{:S(2)}, u32[]{:S(2)}) collective-permute-start(bf16[320,384]{1,0:T(8,128)(2,1)} %get-tuple-element.109), channel_id=1, source_target_pairs={{24,0},{0,8},{8,16},{16,24},{25,1},{1,9},{9,17},{17,25},{26,2},{2,... | collective-permute-start | bytes 737288 | tf_op jit(solution)/shard_map/ppermute | solution.py:949
  285.7 14.1 %collective-permute-start.8 = (bf16[320,384]{1,0:T(8,128)(2,1)}, bf16[320,384]{1,0:T(8,128)(2,1)S(1)}, u32[]{:S(2)}, u32[]{:S(2)}) collective-permute-start(bf16[320,384]{1,0:T(8,128)(2,1)} %get-tuple-element.112), channel_id=1, source_target_pairs={{16,0},{24,8},{0,16},{8,24},{17,1},{25,9},{1,17},{9,25},{18,2},{26... | collective-permute-start | bytes 737288 | tf_op jit(solution)/shard_map/ppermute | solution.py:949
  299.7 12.1 %collective-permute-start.9 = (bf16[320,384]{1,0:T(8,128)(2,1)}, bf16[320,384]{1,0:T(8,128)(2,1)S(1)}, u32[]{:S(2)}, u32[]{:S(2)}) collective-permute-start(bf16[320,384]{1,0:T(8,128)(2,1)} %get-tuple-element.119), channel_id=1, source_target_pairs={{8,0},{16,8},{24,16},{0,24},{9,1},{17,9},{25,17},{1,25},{10,2},{18... | collective-permute-start | bytes 737288 | tf_op jit(solution)/shard_map/ppermute | solution.py:949
  299.8 12.1 %copy-start.5 = (bf16[320,384]{1,0:T(8,128)(2,1)}, bf16[320,384]{1,0:T(8,128)(2,1)S(1)}, u32[]{:S(2)}) copy-start(bf16[320,384]{1,0:T(8,128)(2,1)S(1)} %collective-permute-done.7.refs_1_) | copy-start | bytes 737284
  299.8 12.0 %copy-start.6 = (bf16[320,384]{1,0:T(8,128)(2,1)}, bf16[320,384]{1,0:T(8,128)(2,1)S(1)}, u32[]{:S(2)}) copy-start(bf16[320,384]{1,0:T(8,128)(2,1)S(1)} %collective-permute-done.8.refs_2_) | copy-start | bytes 737284
  311.9 0.7 copy-start.7
  314.7 41.5 %collective-permute-start.10 = (bf16[320,384]{1,0:T(8,128)(2,1)}, bf16[320,384]{1,0:T(8,128)(2,1)S(1)}, u32[]{:S(2)}, u32[]{:S(2)}) collective-permute-start(bf16[320,384]{1,0:T(8,128)(2,1)} %merge.4.refs_0_), channel_id=1, source_target_pairs={{0,1},{1,0},{2,3},{3,2},{4,5},{5,4},{6,7},{7,6},{8,9},{9,8},{10,11... | collective-permute-start | bytes 737288 | tf_op jit(solution)/shard_map/ppermute | solution.py:954
  356.2 0.7 copy-start.9
  358.7 8.4 %collective-permute-start.11 = (bf16[320,384]{1,0:T(8,128)(2,1)}, bf16[320,384]{1,0:T(8,128)(2,1)S(1)}, u32[]{:S(2)}, u32[]{:S(2)}) collective-permute-start(bf16[320,384]{1,0:T(8,128)(2,1)} %merge.5.refs_0_), channel_id=1, source_target_pairs={{0,2},{1,3},{2,0},{3,1},{4,6},{5,7},{6,4},{7,5},{8,10},{9,11},{10,... | collective-permute-start | bytes 737288 | tf_op jit(solution)/shard_map/ppermute | solution.py:954
  367.2 0.7 copy-start.10
  369.7 7.6 %collective-permute-start.12 = (bf16[320,384]{1,0:T(8,128)(2,1)}, bf16[320,384]{1,0:T(8,128)(2,1)S(1)}, u32[]{:S(2)}, u32[]{:S(2)}) collective-permute-start(bf16[320,384]{1,0:T(8,128)(2,1)} %merge.6.refs_0_), channel_id=1, source_target_pairs={{0,4},{1,5},{2,6},{3,7},{4,0},{5,1},{6,2},{7,3},{8,12},{9,13},{10,... | collective-permute-start | bytes 737288 | tf_op jit(solution)/shard_map/ppermute | solution.py:954
  377.3 0.7 copy-start.8
  384.9 8.0 %collective-permute-start.15 = (bf16[152,384]{1,0:T(8,128)(2,1)S(1)}, bf16[152,384]{1,0:T(8,128)(2,1)S(1)}, u32[]{:S(2)}, u32[]{:S(2)}) collective-permute-start(bf16[152,384]{1,0:T(8,128)(2,1)S(1)} %get-tuple-element.167), channel_id=1, source_target_pairs={{8,0},{16,8},{24,16},{0,24},{9,1},{17,9},{25,17},{1,25},{10,2},{18... | collective-permute-start | bytes 350216 | tf_op jit(solution)/shard_map/ppermute | solution.py:949
  386.7 9.6 %collective-permute-start.14 = (bf16[152,384]{1,0:T(8,128)(2,1)S(1)}, bf16[152,384]{1,0:T(8,128)(2,1)S(1)}, u32[]{:S(2)}, u32[]{:S(2)}) collective-permute-start(bf16[152,384]{1,0:T(8,128)(2,1)S(1)} %get-tuple-element.168), channel_id=1, source_target_pairs={{16,0},{24,8},{0,16},{8,24},{17,1},{25,9},{1,17},{9,25},{18,2},{26... | collective-permute-start | bytes 350216 | tf_op jit(solution)/shard_map/ppermute | solution.py:949
  386.7 9.6 %collective-permute-start.13 = (bf16[152,384]{1,0:T(8,128)(2,1)S(1)}, bf16[152,384]{1,0:T(8,128)(2,1)S(1)}, u32[]{:S(2)}, u32[]{:S(2)}) collective-permute-start(bf16[152,384]{1,0:T(8,128)(2,1)S(1)} %get-tuple-element.169), channel_id=1, source_target_pairs={{24,0},{0,8},{8,16},{16,24},{25,1},{1,9},{9,17},{17,25},{26,2},{2,... | collective-permute-start | bytes 350216 | tf_op jit(solution)/shard_map/ppermute | solution.py:949
Sparse Core Ops, SparseCore 0:
  43.2 46.8 all-gather.2
  256.8 90.7 reduce-scatter.1
where the time goes:
time: 424 us; the launch traced here: 422 us
  Pallas kernels  257 us (61%)
  starting transfers between devices  62.2 us (15%)
  waiting for transfers between devices  51 us (12%)
  local copies, waits for them, and re-layouts  20.8 us (5%)
  between operations  15.6 us (4%)
  blocking collectives  10.8 us (3%)
  other arithmetic  4.94 us (1%)
    pallas_call x1, Pallas kernels, relations(): pl.pallas_call(functools.partial(relation_kernel, all_rows=all_rows), gri...  130 us
    pallas_call x4, Pallas kernels, attend_backward(): pl.pallas_call(functools.partial(attend_backward_kernel, share=share), gr...  47 us
    ppermute x4, starting transfers between devices, exchange(): return lax.ppermute(value, 'batch', [(i, i ^ bit) for i in range(size)])  40.3 us
    pallas_call x2, Pallas kernels, attend_forward(): pl.pallas_call(attend_forward_kernel, grid=(count,), in_specs=[SMEM, whol...  32.2 us
    ppermute x12, starting transfers between devices, shift_shares(): lax.ppermute(value, 'heads', [((i + by) % shares, i) for i in range(share...  21.6 us
    all_gather x1, waiting for transfers between devices, body(): parts_all = lax.all_gather(parts, 'batch', axis=0)  20.3 us
    pallas_call x1, Pallas kernels, block_backward(): pl.pallas_call(block_backward_kernel, grid=(rows // tile,), in_specs=[SME...  19.7 us
    ppermute x4, waiting for transfers between devices, exchange(): return lax.ppermute(value, 'batch', [(i, i ^ bit) for i in range(size)])  18.9 us
  transfers between devices with their start and end apart: 18, of which 7 were waited for; matrix products, arithmetic and copies ran while one was open for 3% of the time, Pallas kernels for 21%

commit v1 on v0

--- a/solution.py
+++ b/solution.py
@@ -91,6 +91,32 @@
 def step_place(step, tile, per_head):
     head = step // per_head
     return head, pl.ds(pl.multiple_of(lax.rem(step, per_head) * tile, tile), tile)
+
+
+def skew(first, second):
+    steps = [first[0]]
+    for index in range(1, len(first)):
+        steps += [first[index], second[index - 1]]
+    return steps + [second[-1]]
+
+
+def run_rolled(steps, logits, vector, back, reset=None, enter=None):
+    def pair(index, carry):
+        for slot in range(2):
+            step = 2 * index + slot
+            if enter is not None:
+                enter(step, slot, index)
+            ahead = logits(jnp.minimum(step + 1, steps - 1), 1 - slot)
+            weave(ahead + back(jnp.maximum(step - 1, 0), 1 - slot), vector(step, slot))
+            if slot == 0 and reset is not None:
+                pl.when(index == 0)(reset)
+        return carry
+
+    for chunk in logits(jnp.int32(0), 0):
+        chunk()
+    lax.fori_loop(0, steps // 2, pair, 0)
+    for chunk in back(jnp.int32(steps - 1), 1):
+        chunk()
 
 
 def run_pipeline(steps, logits, vector, back, enter=None):
@@ -277,7 +303,7 @@
     grads = r_ref[...] * d_ref[...].astype(f32)
     shifts = grads * a_ref[...].astype(f32)
     k = k_ref[...].astype(f32)
-    for head in range(PART):
+    def one_head(head, carry):
         inside = in_head(lane, head)
         shift = -jnp.sum(jnp.where(inside, shifts, 0.0), axis=1, keepdims=True)
         high = shift.astype(bf16).astype(f32)
@@ -285,13 +311,20 @@
             grads, head, HEAD_DIM, jnp.where(lane == 96, high, jnp.where(lane == 97, shift - high, 0.0))
         )
         keys[head] = jnp.where(inside, k, 0.0).astype(bf16)
+        return carry
+
+    lax.fori_loop(0, PART, one_head, 0)
     rhs[:, :128] = jnp.where((lane == 96) | (lane == 97), 1.0, v_ref[...].astype(f32)).astype(bf16)
     rhs[:, 128:] = v_ref[...]
     qt[...] = q_ref[...].T
     dt[...] = grads.astype(bf16).T
-    dq[...] = jnp.zeros_like(dq)
-    dkt[...] = jnp.zeros_like(dkt)
-    dvt[...] = jnp.zeros_like(dvt)
+
+    def reset():
+        dq[...] = jnp.zeros_like(dq)
+        dkt[...] = jnp.zeros_like(dkt)
+        dvt[...] = jnp.zeros_like(dvt)
+
+    reset()
 
     def logits(step, slot):
         head, span = step_place(step, tile, per_head)
@@ -399,248 +432,338 @@
 
 
 def relation_kernel(
-    length_ref, split_ref, block_ref, teacher_ref, own_ref, packed_ref, small_ref, d_ref, g_ref, kl_ref, pack, ls, rs, lt, rt, keys, left_t, zs, zt, gs, left_sum, right_t, es_all, et_all, weight, grads_s,
-    *, all_rows,
+    length_ref, split_ref, block_ref, teacher_ref, own_ref, packed_ref, small_ref, d_ref, g_ref, kl_ref, kl_row_ref,
+    pack, lefts, rights, t_lefts, t_rights, ls, rs, lt, rt, keys, left_t, zs0, zs1, zt0, zt1, gs0, gs1,
+    left_sum, right_t, es_all, et_all, parts, columns, factors, rows_s, weight, weight_row, grads_s, *, all_rows,
 ):
     rows = block_ref.shape[0]
-    tile = zs.shape[1]
+    tile = zs0.shape[0]
     per_head = rows // tile
     steps = PART * per_head
+    zs, zt, gs = (zs0, zs1), (zt0, zt1), (gs0.at[:tile], gs1)
     length, split = own_number(length_ref), own_number(split_ref)
-    block = block_ref[...]
-    teacher = teacher_ref[...]
+
     @pl.when(pl.program_id(0) == 0)
     def _():
         pack[...] = own_ref[...]
+        position = lax.broadcasted_iota(jnp.int32, (rows, 1), 0)
+        counted = (position < length) & (position != 0) & (position != split - 1) & (position != length - 1)
+        share = 1.0 / ((length - 3).astype(f32) * float(all_rows))
+        weight[...] = jnp.where(counted, share, 0.0)
+        position = lanes((1, rows))
+        counted = (position < length) & (position != 0) & (position != split - 1) & (position != length - 1)
+        weight_row[...] = jnp.where(counted, share, 0.0)
+        kl_ref[...] = jnp.zeros_like(kl_ref)
+        kl_row_ref[...] = jnp.zeros_like(kl_row_ref)
+        d_ref[...] = jnp.zeros_like(d_ref)
 
     @pl.when(pl.program_id(0) > 0)
     def _():
         unpack(packed_ref, 0, pack, MID_ROWS)
 
-    w_ref, g_ref = pack, g_ref.at[0]
+    g_ref = g_ref.at[0]
     small = small_ref[0].astype(f32)
-    lane = lanes((rows, 128))
-    position = lax.broadcasted_iota(jnp.int32, (rows, 1), 0)
-    bias = key_bias(rows, length)
-
-    @pl.when(pl.program_id(0) == 0)
-    def _():
-        counted = (position < length) & (position != 0) & (position != split - 1) & (position != length - 1)
-        share = 1.0 / ((length - 3).astype(f32) * float(all_rows))
-        weight[...] = jnp.where(counted, share, 0.0)
-        kl_ref[...] = jnp.zeros_like(kl_ref)
-        d_ref[...] = jnp.zeros_like(d_ref)
-
-    def teacher_part(index, b):
-        start = 288 + index * 192
-        flat = dot(teacher[:, :D], pack[start : start + 192, :], NT)
-        flat = flat + dot(teacher[:, D:], pack[start + 576 : start + 768, :], NT)
-        if b is not None:
-            flat = flat + b
-        flat = flat.astype(bf16)
-        return flat[:, :128], wide_rows(flat[:, 128:])
-
-    def largest(rows_low, size, blocks):
-        square = rows_low.astype(f32)
-        square = (square * square).astype(bf16)
-        feature = lax.broadcasted_iota(jnp.int32, (128, 128), 0) // size
-        same = feature == lanes((128, 128)) // size
-        return jnp.max(dot(square, jnp.where(same, 1.0, 0.0).astype(bf16)), axis=0, keepdims=True)
-
-    def relate(left, right, t_left, t_right, symmetric):
+
+    def largest(low, size):
+        square = low.astype(f32)
+        same = lax.broadcasted_iota(jnp.int32, (128, 128), 0) // size == lanes((128, 128)) // size
+        return jnp.max(dot((square * square).astype(bf16), jnp.where(same, 1.0, 0.0).astype(bf16)), axis=0, keepdims=True)
+
+    def project(index, carry):
+        here = pl.ds(pl.multiple_of(index * tile, tile), tile)
+        block, teacher = block_ref[here, :], teacher_ref[here, :]
+
+        def student(part, b):
+            flat = dot(block, pack[part * 96 : (part + 1) * 96, :], NT)
+            return wide_rows(flat if b is None else flat + b).astype(bf16)
+
+        def taught(part, b):
+            start = 288 + part * 192
+            flat = dot(teacher[:, :D], pack[start : start + 192, :], NT)
+            flat = flat + dot(teacher[:, D:], pack[start + 576 : start + 768, :], NT)
+            flat = (flat if b is None else flat + b).astype(bf16)
+            return flat[:, :128], wide_rows(flat[:, 128:])
+
+        q, k, v = student(0, small[2:3, :96]), student(1, None), student(2, small[3:4, :96])
+        lefts[0, here, :] = q
+        rights[0, here, :] = k
+        lefts[1, here, :] = v
+        rights[1, here, :] = v
+        tq, tk, tv = taught(0, small[5:6, :192]), taught(1, None), taught(2, small[6:7, :192])
+        for half in range(2):
+            t_lefts[0, half, here, :] = tq[half]
+            t_rights[0, half, here, :] = tk[half]
+            t_lefts[1, half, here, :] = tv[half]
+            t_rights[1, half, here, :] = tv[half]
+        found = [largest(value, HEAD_DIM) for value in (q, k, v)]
+        found += [largest(value, TEACHER_HEAD_DIM) for value in tq + tk + tv]
+        return tuple(jnp.maximum(old, new) for old, new in zip(carry, found))
+
+    top = lax.fori_loop(0, rows // tile, project, (jnp.zeros((1, 128), f32),) * 9)
+    bounds = []
+    for s_left, s_right, t_left, t_right in ((0, 1, 3, 5), (2, 2, 7, 7)):
+        bound = jnp.max(top[s_left] * top[s_right]) * STUDENT_LOG**2
+        for half in range(2):
+            bound = jnp.maximum(bound, jnp.max(top[t_left + half] * top[t_right + half]) * TEACHER_LOG**2)
+        bounds.append(bound)
+
+    def operands(relation, student_scale, teacher_scale, row_bias, everything):
+        band = min(128, rows)
+        line = lanes((1, 128))
+
+        def terms(value, inside, extra):
+            high, low = value
+            return jnp.where(inside, high, extra).astype(bf16), jnp.where(inside, low, 0.0).astype(bf16)
+
+        def halves(value, scale):
+            value = value * scale
+            high = value.astype(bf16).astype(f32)
+            return high, value - high
+
+        def one_band(index, carry):
+            here = pl.ds(pl.multiple_of(index * band, band), band)
+            position = lax.broadcasted_iota(jnp.int32, (band, 128), 0) + index * band
+            bias = jnp.where(position < length, 0.0, MASKED)
+            row = jnp.where(row_bias, bias, 0.0)
+            left, right = lefts[relation, here, :].astype(f32), rights[relation, here, :].astype(f32)
+            value = halves(left, student_scale)
+            extra = jnp.where(line == 97, row, jnp.where(line == 96, 1.0, 0.0))
+            if everything:
+                rs[here, :128] = jnp.where(line == 97, 1.0, jnp.where(line == 96, bias, right)).astype(bf16)
+                rs[here, 128:] = rights[relation, here, :]
+            for head in range(PART):
+                inside = in_head(line, head)
+                ls[head, here, :128], ls[head, here, 128:] = terms(value, inside, extra)
+                if everything:
+                    keys[head, here, :] = jnp.where(inside, right, 0.0).astype(bf16)
+            for half in range(2):
+                t_left = t_lefts[relation, half, here, :].astype(f32)
+                t_right = t_rights[relation, half, here, :].astype(f32)
+                value = halves(t_left, teacher_scale)
+                for head in range(2 * half, min(2 * half + 2, PART)):
+                    own = head % 2
+                    spare = (1 - own) * TEACHER_HEAD_DIM
+                    extra = jnp.where(line == spare + 1, row, jnp.where(line == spare, 1.0, 0.0))
+                    inside = in_head(line, own, TEACHER_HEAD_DIM)
+                    lt[head, here, :128], lt[head, here, 128:] = terms(value, inside, extra)
+                    if everything:
+                        first = jnp.where(line == spare + 1, 1.0, jnp.where(line == spare, bias, t_right))
+                        rt[head, here, :128] = first.astype(bf16)
+                        rt[head, here, 128:] = t_rights[relation, half, here, :]
+            return carry
+
+        lax.fori_loop(0, rows // band, one_band, 0)
+
+    def relate(relation, carry):
+        symmetric = relation == 1
+        left_t[...] = lefts[relation].T
+        operands(relation, STUDENT_LOG, TEACHER_LOG, symmetric, True)
+        near = jnp.where(symmetric, bounds[1], bounds[0]) < SAFE * SAFE
+        reset()
+
+        @pl.when(near & jnp.logical_not(symmetric))
+        def _():
+            run_pipeline(steps, logits, vector, grad_products)
+
+        @pl.when(near & symmetric)
+        def _():
+            lax.fori_loop(0, PART, symmetric_head, 0)
+
+        @pl.when(jnp.logical_not(near))
+        def _():
+            operands(relation, 1.0, 1.0, False, False)
+            lax.fori_loop(0, steps, shifted_step, 0)
+
+        @pl.when(jnp.logical_not(symmetric))
+        def _():
+            grads_s[0] = (left_sum[...] * STUDENT_SCALE).astype(bf16)
+            grads_s[1] = (right_t[...] * STUDENT_SCALE).T.astype(bf16)
+
+        @pl.when(symmetric)
+        def _():
+            grads_s[2] = ((left_sum[...] + right_t[...].T) * STUDENT_SCALE).astype(bf16)
+
+        return carry
+
+    def reset():
         left_sum[...] = jnp.zeros_like(left_sum)
         right_t[...] = jnp.zeros_like(right_t)
-        left_t[...] = left.T
-        left_wide = left.astype(f32) * STUDENT_LOG
-        right_wide = right.astype(f32)
-        one = jnp.where(lane == 96, 1.0, 0.0)
-        if symmetric:
-            one = jnp.where(lane == 97, bias, one)
-        first = jnp.where(lane == 96, bias, right_wide)
-        if symmetric:
-            first = jnp.where(lane == 97, 1.0, first)
-        rs[:, :128] = first.astype(bf16)
-        rs[:, 128:] = right
-        for head in range(PART):
-            ls[head] = split_terms(left_wide, head, HEAD_DIM, one)
-            keys[head] = jnp.where(in_head(lane, head), right_wide, 0.0).astype(bf16)
-            own = head % 2
-            spare = (1 - own) * TEACHER_HEAD_DIM
-            one_t = jnp.where(lane == spare, 1.0, 0.0)
-            wide_t = t_right[head // 2].astype(f32)
-            first_t = jnp.where(lane == spare, bias, wide_t)
-            if symmetric:
-                one_t = jnp.where(lane == spare + 1, bias, one_t)
-                first_t = jnp.where(lane == spare + 1, 1.0, first_t)
-            lt[head] = split_terms(t_left[head // 2].astype(f32) * TEACHER_LOG, own, TEACHER_HEAD_DIM, one_t)
-            rt[head, :, :128] = first_t.astype(bf16)
-            rt[head, :, 128:] = t_right[head // 2]
-        student_bound = largest(left, HEAD_DIM, 4) * largest(right, HEAD_DIM, 4) * STUDENT_LOG**2
-        bound = jnp.max(student_bound)
-        for part in range(2):
-            t_bound = largest(t_left[part], TEACHER_HEAD_DIM, 2) * largest(t_right[part], TEACHER_HEAD_DIM, 2)
-            bound = jnp.maximum(bound, jnp.max(t_bound * TEACHER_LOG**2))
-        near = bound < SAFE * SAFE
-
-        @pl.when(near)
-        def _():
-            if symmetric:
-                symmetric_pass()
-            else:
-                plain_pass()
-
-        @pl.when(jnp.logical_not(near))
-        def _():
-            for head in range(PART):
-                own = head % 2
-                spare = (1 - own) * TEACHER_HEAD_DIM
-                ls[head] = split_terms(left.astype(f32), head, HEAD_DIM, jnp.where(lane == 96, 1.0, 0.0))
-                lt[head] = split_terms(
-                    t_left[head // 2].astype(f32), own, TEACHER_HEAD_DIM, jnp.where(lane == spare, 1.0, 0.0)
-                )
-            shifted_pass()
-
-    def plain_pass():
-        def logits(step, slot):
-            head, span = step_place(step, tile, per_head)
-
-            def student(start):
-                zs[slot, :, start : start + 256] = dot(ls[head, span, :], rs[start : start + 256, :], NT)
-
-            def taught(start):
-                zt[slot, :, start : start + 256] = dot(lt[head, span, :], rt[head, start : start + 256, :], NT)
-
-            chunks = []
-            for start in range(0, rows, 256):
-                chunks += [functools.partial(student, start), functools.partial(taught, start)]
-            return chunks
-
-        def vector(step, slot):
-            base = lax.rem(step, per_head) * tile
-
-            def strip(start):
-                here = pl.ds(pl.multiple_of(base + start, STRIP), STRIP)
-                student = zs[slot, start : start + STRIP, :]
-                taught = zt[slot, start : start + STRIP, :]
-                es = jnp.exp2(student)
-                et = jnp.exp2(taught)
-                sum_s = row_sum(es)
-                sum_t = row_sum(et)
-                cross = row_sum(et * (taught - student))
-                w = weight[here, :]
-                inverse = 1.0 / sum_t
-                kl_ref[here, :] += w * (LN2 * cross * inverse + jnp.log(sum_s) - jnp.log(sum_t))
-                gs[slot, start : start + STRIP, :] = (es * (w / sum_s) - et * (w * inverse)).astype(bf16)
-
-            return [functools.partial(strip, start) for start in range(0, tile, STRIP)]
-
-        run_pipeline(steps, logits, vector, grad_products)
+
+    def logits(step, slot):
+        head, span = step_place(step, tile, per_head)
+
+        def student(start):
+            zs[slot][:, start : start + 256] = dot(ls[head, span, :], rs[start : start + 256, :], NT)
+
+        def taught(start):
+            zt[slot][:, start : start + 256] = dot(lt[head, span, :], rt[head, start : start + 256, :], NT)
+
+        chunks = []
+        for start in range(0, rows, 256):
+            chunks += [functools.partial(student, start), functools.partial(taught, start)]
+        return chunks
+
+    def vector(step, slot):
+        base = lax.rem(step, per_head) * tile
+        z, t, g = zs[slot], zt[slot], gs[slot]
+        scales = {}
+
+        def weigh(start):
+            strip = slice(start, start + STRIP)
+            sum_s = sum_t = cross = 0.0
+            for column in range(0, rows, 128):
+                part = slice(column, column + 128)
+                student, taught = z[strip, part], t[strip, part]
+                es, et = jnp.exp2(student), jnp.exp2(taught)
+                z[strip, part] = es
+                t[strip, part] = et
+                sum_s, sum_t, cross = sum_s + es, sum_t + et, cross + et * (taught - student)
+            here = pl.ds(pl.multiple_of(base + start, STRIP), STRIP)
+            sum_s, sum_t, cross = (jnp.sum(v, axis=1, keepdims=True) for v in (sum_s, sum_t, cross))
+            w = weight[here, :]
+            inverse = 1.0 / sum_t
+            kl_ref[here, :] += w * (LN2 * cross * inverse + jnp.log(sum_s) - jnp.log(sum_t))
+            scales[start] = w / sum_s, w * inverse
+
+        def grad(start):
+            strip = slice(start, start + STRIP)
+            a, b = scales[start]
+            for column in range(0, rows, 128):
+                part = slice(column, column + 128)
+                g[strip, part] = (z[strip, part] * a - t[strip, part] * b).astype(bf16)
+
+        starts = range(0, tile, STRIP)
+        return skew([functools.partial(weigh, s) for s in starts], [functools.partial(grad, s) for s in starts])
 
     def grad_products(step, slot):
         head, span = step_place(step, tile, per_head)
         own = pl.ds(pl.multiple_of(head * HEAD_DIM, HEAD_DIM), HEAD_DIM)
 
         def first():
-            left_sum[span, :] += dot(gs[slot], keys[head])
+            left_sum[span, :] += dot(gs[slot][...], keys[head])
 
         def second(start):
             part = slice(start, start + 256)
-            right_t[own, part] += dot(left_t[own, span], gs[slot, :, part])
+            right_t[own, part] += dot(left_t[own, span], gs[slot][:, part])
 
         return [first] + [functools.partial(second, start) for start in range(0, rows, 256)]
 
-    def shifted_pass():
-        def one(step, carry):
-            head, span = step_place(step, tile, per_head)
-            student = dot(ls[head, span, :], rs[...], NT)
-            student = (student - jnp.max(student, axis=1, keepdims=True)) * STUDENT_LOG
-            taught = dot(lt[head, span, :], rt[head], NT)
-            taught = (taught - jnp.max(taught, axis=1, keepdims=True)) * TEACHER_LOG
-            es = jnp.exp2(student)
-            et = jnp.exp2(taught)
-            sum_s = jnp.sum(es, axis=1, keepdims=True)
-            sum_t = jnp.sum(et, axis=1, keepdims=True)
-            cross = jnp.sum(et * (taught - student), axis=1, keepdims=True)
-            w = weight[span, :]
+    def shifted_step(step, carry):
+        head, span = step_place(step, tile, per_head)
+        student = dot(ls[head, span, :], rs[...], NT)
+        zs0[...] = (student - jnp.max(student, axis=1, keepdims=True)) * STUDENT_LOG
+        taught = dot(lt[head, span, :], rt[head], NT)
+        zt0[...] = (taught - jnp.max(taught, axis=1, keepdims=True)) * TEACHER_LOG
+
+        def strip(index, carry):
+            here = pl.ds(pl.multiple_of(index * STRIP, STRIP), STRIP)
+            student, taught = zs0[here, :], zt0[here, :]
+            es, et = jnp.exp2(student), jnp.exp2(taught)
+            sum_s, sum_t = row_sum(es), row_sum(et)
+            cross = row_sum(et * (taught - student))
+            there = pl.ds(pl.multiple_of(lax.rem(step, per_head) * tile + index * STRIP, STRIP), STRIP)
+            w = weight[there, :]
             row = LN2 * cross / sum_t + jnp.log(sum_s) - jnp.log(sum_t)
-            kl_ref[span, :] += jnp.where(w > 0.0, w * row, 0.0)
-            gs[0] = (es * (w / sum_s) - et * (w / sum_t)).astype(bf16)
-            for chunk in grad_products(step, 0):
-                chunk()
+            kl_ref[there, :] += jnp.where(w > 0.0, w * row, 0.0)
+            gs0[here, :] = (es * (w / sum_s) - et * (w / sum_t)).astype(bf16)
             return carry
 
-        lax.fori_loop(0, steps, one, 0)
-
-    def symmetric_pass():
-        size = min(256, rows)
+        lax.fori_loop(0, tile // STRIP, strip, 0)
+        for chunk in grad_products(step, 0):
+            chunk()
+        return carry
+
+    def symmetric_head(head, carry):
+        size, band = min(256, rows), 32
         count = rows // size
-
-        def column(row):
-            return jnp.broadcast_to(row, (128, size)).T[:, :1]
-
-        def row_of(value):
-            return jnp.broadcast_to(value, (size, 128)).T[:1, :]
-
-        def one_head(head, carry):
-            own = pl.ds(pl.multiple_of(head * HEAD_DIM, HEAD_DIM), HEAD_DIM)
-            by_row = []
-            by_column = [[jnp.zeros((1, size), f32)] * 3 for _ in range(count)]
-            for i in range(count):
-                here = slice(i * size, (i + 1) * size)
-                after = slice(i * size, rows)
-                student = dot(ls[head, here, :], rs[after, :], NT)
-                taught = dot(lt[head, here, :], rt[head, after, :], NT)
-                es = jnp.exp2(student)
-                et = jnp.exp2(taught)
-                cross = et * (taught - student)
-                es_all[here, after] = es
-                et_all[here, after] = et
-                by_row.append([row_sum(t) for t in (es, et, cross)])
-                for j in range(i + 1, count):
-                    part = slice((j - i) * size, (j - i + 1) * size)
-                    by_column[j] = [
-                        c + jnp.sum(t[:, part], axis=0, keepdims=True)
-                        for c, t in zip(by_column[j], (es, et, cross))
-                    ]
-            a, b = [], []
-            for i in range(count):
-                here = slice(i * size, (i + 1) * size)
-                sum_s, sum_t, cross = (r + column(c) for r, c in zip(by_row[i], by_column[i]))
-                w = weight[here, :]
-                sum_s = jnp.where(w > 0.0, sum_s, 1.0)
-                sum_t = jnp.where(w > 0.0, sum_t, 1.0)
-                inverse = 1.0 / sum_t
-                kl_ref[here, :] += w * (LN2 * cross * inverse + jnp.log(sum_s) - jnp.log(sum_t))
-                a.append(w / sum_s)
-                b.append(w * inverse)
-            a_row = jnp.concatenate([row_of(t) for t in a], axis=1)
-            b_row = jnp.concatenate([row_of(t) for t in b], axis=1)
-            for i in range(count):
-                here = slice(i * size, (i + 1) * size)
-                after = slice(i * size, rows)
-                both = es_all[here, after] * (a[i] + a_row[:, after])
-                both = (both - et_all[here, after] * (b[i] + b_row[:, after])).astype(bf16)
-                left_sum[here, :] += dot(both, keys[head, after, :])
-                if i + 1 < count:
-                    right_t[own, (i + 1) * size :] += dot(left_t[own, here], both[:, size:])
-            return carry
-
-        lax.fori_loop(0, PART, one_head, 0)
-
-    q = project_part(block, w_ref, 0, small[2:3, :96])
-    k = project_part(block, w_ref, 1, None)
-    tq = teacher_part(0, small[5:6, :192])
-    tk = teacher_part(1, None)
-    relate(q, k, tq, tk, False)
-    grads_s[0] = (left_sum[...] * STUDENT_SCALE).astype(bf16)
-    grads_s[1] = (right_t[...] * STUDENT_SCALE).T.astype(bf16)
-    v = project_part(block, w_ref, 2, small[3:4, :96])
-    tv = teacher_part(2, small[6:7, :192])
-    relate(v, v, tv, tv, True)
-    grads_s[2] = ((left_sum[...] + right_t[...].T) * STUDENT_SCALE).astype(bf16)
+        own = pl.ds(pl.multiple_of(head * HEAD_DIM, HEAD_DIM), HEAD_DIM)
+        columns[...] = jnp.zeros_like(columns)
+
+        def logit_chunks(i):
+            here = slice(i * size, (i + 1) * size)
+
+            def student(part):
+                es_all[here, part] = dot(ls[head, here, :], rs[part, :], NT)
+
+            def taught(part):
+                et_all[here, part] = dot(lt[head, here, :], rt[head, part, :], NT)
+
+            chunks = []
+            for j in range(i, count):
+                part = slice(j * size, (j + 1) * size)
+                chunks += [functools.partial(student, part), functools.partial(taught, part)]
+            return chunks
+
+        def weigh(i, start):
+            strip = slice(start, start + band)
+            totals = [0.0, 0.0, 0.0]
+            for column in range(i * size, rows, 128):
+                part = slice(column, column + 128)
+                student, taught = es_all[strip, part], et_all[strip, part]
+                es, et = jnp.exp2(student), jnp.exp2(taught)
+                es_all[strip, part] = es
+                et_all[strip, part] = et
+                for index, value in enumerate((es, et, et * (taught - student))):
+                    totals[index] = totals[index] + value
+                    if column >= (i + 1) * size:
+                        eight = value[:8]
+                        for line in range(8, band, 8):
+                            eight = eight + value[line : line + 8]
+                        columns[index, :, part] += eight
+            for index in range(3):
+                parts[index, strip, :] = totals[index]
+
+        def combine(i, start):
+            strip = slice(start, start + STRIP)
+            a, b = factors[0, strip, :], factors[1, strip, :]
+            for column in range(i * size, rows, 128):
+                part = slice(column, column + 128)
+                both = es_all[strip, part] * (a + rows_s[0, :, part])
+                both = both - et_all[strip, part] * (b + rows_s[1, :, part])
+                gs0[strip, part] = both.astype(bf16)
+
+        def products(i):
+            here = slice(i * size, (i + 1) * size)
+
+            def first(j):
+                part = slice(j * size, (j + 1) * size)
+                left_sum[here, :] += dot(gs_all[here, part], keys[head, part, :])
+
+            def second(j):
+                part = slice(j * size, (j + 1) * size)
+                right_t[own, part] += dot(left_t[own, here], gs_all[here, part])
+
+            chunks = [functools.partial(first, j) for j in range(i, count)]
+            return chunks + [functools.partial(second, j) for j in range(i + 1, count)]
+
+        gs_all = gs0
+        for chunk in logit_chunks(0):
+            chunk()
+        for i in range(count):
+            ahead = logit_chunks(i + 1) if i + 1 < count else []
+            weave(ahead, [functools.partial(weigh, i, s) for s in range(i * size, (i + 1) * size, band)])
+        sums = [
+            jnp.sum(parts[index].T, axis=0, keepdims=True) + jnp.sum(columns[index], axis=0, keepdims=True)
+            for index in range(3)
+        ]
+        w = weight_row[...]
+        sum_s, sum_t = (jnp.where(w > 0.0, value, 1.0) for value in sums[:2])
+        inverse = 1.0 / sum_t
+        kl_row_ref[...] += w * (LN2 * sums[2] * inverse + jnp.log(sum_s) - jnp.log(sum_t))
+        for index, value in enumerate((w / sum_s, w * inverse)):
+            factors[index] = jnp.broadcast_to(value, (128, rows)).T
+            rows_s[index] = jnp.broadcast_to(value, (STRIP, rows))
+        for i in range(count):
+            behind = products(i - 1) if i else []
+            weave(behind, [functools.partial(combine, i, s) for s in range(i * size, (i + 1) * size, STRIP)])
+        for chunk in products(count - 1):
+            chunk()
+        return carry
+
+    lax.fori_loop(0, 2, relate, 0)
     grads = tuple(grads_s[i] for i in range(3))
-    weight_grads(grads, block, g_ref)
-    d_ref[...] += spread(grads, w_ref)
+    weight_grads(grads, block_ref[...], g_ref)
+    d_ref[...] += spread(grads, pack)
 
 
 def part_rows(rows, batch):
@@ -671,28 +794,41 @@
         in_specs=[
             SMEM, SMEM, whole(block.shape), whole(teacher.shape), whole(own.shape), place, share(small.shape),
         ],
-        out_specs=[whole(block.shape), share((shares, 320, D)), whole((rows, 1))],
+        out_specs=[whole(block.shape), share((shares, 320, D)), whole((rows, 1)), whole((1, rows))],
         out_shape=[
             jax.ShapeDtypeStruct(block.shape, f32),
             jax.ShapeDtypeStruct((shares, 320, D), bf16),
             jax.ShapeDtypeStruct((rows, 1), f32),
+            jax.ShapeDtypeStruct((1, rows), f32),
         ],
         scratch_shapes=[
             pltpu.VMEM((1440, D), bf16),
+            pltpu.VMEM((2, rows, 128), bf16),
+            pltpu.VMEM((2, rows, 128), bf16),
+            pltpu.VMEM((2, 2, rows, 128), bf16),
+            pltpu.VMEM((2, 2, rows, 128), bf16),
             pltpu.VMEM((PART, rows, 256), bf16),
             pltpu.VMEM((rows, 256), bf16),
             pltpu.VMEM((PART, rows, 256), bf16),
             pltpu.VMEM((PART, rows, 256), bf16),
             pltpu.VMEM((PART, rows, 128), bf16),
             pltpu.VMEM((128, rows), bf16),
-            pltpu.VMEM((2, tile, rows), f32),
-            pltpu.VMEM((2, tile, rows), f32),
-            pltpu.VMEM((2, tile, rows), bf16),
+            pltpu.VMEM((tile, rows), f32),
+            pltpu.VMEM((tile, rows), f32),
+            pltpu.VMEM((tile, rows), f32),
+            pltpu.VMEM((tile, rows), f32),
+            pltpu.VMEM((rows, rows), bf16),
+            pltpu.VMEM((tile, rows), bf16),
             pltpu.VMEM((rows, 128), f32),
             pltpu.VMEM((128, rows), f32),
             pltpu.VMEM((rows, rows), f32),
             pltpu.VMEM((rows, rows), f32),
+            pltpu.VMEM((3, rows, 128), f32),
+            pltpu.VMEM((3, 8, rows), f32),
+            pltpu.VMEM((2, rows, 128), f32),
+            pltpu.VMEM((2, STRIP, rows), f32),
             pltpu.VMEM((rows, 1), f32),
+            pltpu.VMEM((1, rows), f32),
             pltpu.VMEM((3, rows, 128), bf16),
         ],
         compiler_params=pltpu.CompilerParams(vmem_limit_bytes=VMEM),
@@ -823,7 +959,7 @@
 
 def block_backward_kernel(
     length_ref, d_ref, n1_ref, r1_ref, n2_ref, r2_ref, act_ref, slope_ref, own_ref, packed_ref, gain_ref,
-    shift_ref, kl_ref, square_ref, six_ref, first_ref, other_ref, *rest,
+    shift_ref, kl_ref, kl_row_ref, square_ref, six_ref, first_ref, other_ref, *rest,
 ):
     step = pl.program_id(0)
     pack = rest[-1]
@@ -887,7 +1023,7 @@
             g_ref[2 * units + 128 :, own] = six_ref[s]
             first = lax.broadcasted_iota(jnp.int32, (32, units), 0) == 0
             g_ref[2 * units + 96 : 2 * units + 128, own] = jnp.where(first, g_sum[s : s + 1, :], 0.0).astype(bf16)
-        scalars = [jnp.sum(kl_ref[...], axis=0, keepdims=True)]
+        scalars = [jnp.sum(kl_ref[...], axis=0, keepdims=True) + jnp.sum(kl_row_ref[...], axis=1, keepdims=True)]
         scalars += [jnp.sum(square_ref[i : i + 1, :], axis=1, keepdims=True) for i in range(3)]
         scalars += [jnp.broadcast_to(own_number(length_ref).astype(f32), (1, 1))]
         lane = lanes((8, width))
@@ -912,7 +1048,7 @@
         grid=(rows // tile,),
         in_specs=[
             SMEM, row, row, column, row, column, whole(act.shape), by_tile(tile, shares * units), whole(own.shape), mid_part(packed), whole(gain.shape), whole(shift.shape),
-            whole(divergence.shape), whole(squares.shape), whole(six.shape),
+            whole(divergence[0].shape), whole(divergence[1].shape), whole(squares.shape), whole(six.shape),
         ] + [whole(a.shape) for a in attended],
         out_specs=[
             row, *[by_tile(tile, 128)] * shares, whole((2 * units + 448, shares * width)), whole((32, width)),
@@ -936,7 +1072,7 @@
         cost_estimate=cost(25),
         name="block_backward",
     )(
-        length, d_block, n1, r1, n2, r2, act, slope, own, packed, gain, shift, divergence, squares, six, *attended
+        length, d_block, n1, r1, n2, r2, act, slope, own, packed, gain, shift, *divergence, squares, six, *attended
     )
 
 
@@ -1060,7 +1196,7 @@
     block, n1, r1, n2, r2, act, slope, squares = block_forward(
         valid_length, x, attended, mid, parts_all, smalls, branch_bias, norm_gain, norm_bias
     )
-    d_block, g_six, divergence = relations(
+    d_block, g_six, *divergence = relations(
         valid_length, split_point, block, teacher, rest, parts_all, smalls, all_rows
     )
     result = block_backward(
@@ -1086,15 +1222,18 @@
     five_sum = merge(g_five)
     both = after(both, five_sum)
     both = to_owner([both[:, s * D : (s + 1) * D] for s in range(shares)])
-    bit = 1
-    while 2 * bit < batch:
-        five_sum = merge([five_sum, exchange(five_sum, bit)])
-        if bit == 1:
+    bits = [1 << i for i in range(batch.bit_length() - 1)]
+    for index, bit in enumerate(bits):
+        received = exchange(five_sum, bit)
+        if index == 1:
             both = [after(p, five_sum) for p in both]
-        bit *= 2
-    both = sum(p.astype(f32) for p in both).astype(bf16)
-    both = lax.all_gather(both, "batch", axis=0, tiled=True)
-    grad_five, five_sums = merge([five_sum, exchange(five_sum, bit)], last=True)
+            both = sum(p.astype(f32) for p in both).astype(bf16)
+            five_sum = after(five_sum, both)
+        if index == len(bits) - 1:
+            both = lax.all_gather(after(both, five_sum), "batch", axis=0, tiled=True)
+            five_sum = after(five_sum, both)
+        five_sum = merge([five_sum, received], last=index == len(bits) - 1)
+    grad_five, five_sums = five_sum
     grad_narrow, grad_wide, grad_out, wide_bias, grad_six, six_sums = finish_mid(both)
     totals = five_sums[8]
     counted = totals[4] * D

time: 424 us -> 696 us (1.64)
  Pallas kernels: 257 us -> 490 us
  waiting for transfers between devices: 51 us -> 113 us
  starting transfers between devices: 62.2 us -> 30.7 us
    pallas_call x1, Pallas kernels: 130 us -> 362 us  [relations(): pl.pallas_call(functools.partial(relation_kernel, all_rows=all_rows), gri...]
    reduce_scatter x1, waiting for transfers between devices: 0.01 us -> 77.7 us  [body(): both = lax.psum_scatter(g_both, 'batch', scatter_dimension=0, tiled=True)]
    ppermute x4, starting transfers between devices: 40.3 us -> 11 us  [exchange(): return lax.ppermute(value, 'batch', [(i, i ^ bit) for i in range(size)])]
    ppermute x4, waiting for transfers between devices: 18.9 us -> 1.89 us  [exchange(): return lax.ppermute(value, 'batch', [(i, i ^ bit) for i in range(size)])]
  transfers between devices with their start and end apart: 18 -> 18, of which waited for: 7 -> 6; matrix products, arithmetic and copies ran while one was open for 3% -> 1% of each run, Pallas kernels for 21% -> 13%
where the time goes in v1:
time: 696 us; the launch traced here: 688 us
  Pallas kernels  490 us (70%)
  waiting for transfers between devices  113 us (16%)
  starting transfers between devices  30.7 us (4%)
  local copies, waits for them, and re-layouts  20.8 us (3%)
  between operations  15.3 us (2%)
  blocking collectives  13 us (2%)
    pallas_call x1, Pallas kernels, relations(): pl.pallas_call(functools.partial(relation_kernel, all_rows=all_rows), gri...  362 us
    reduce_scatter x1, waiting for transfers between devices, body(): both = lax.psum_scatter(g_both, 'batch', scatter_dimension=0, tiled=True)  77.7 us
    pallas_call x4, Pallas kernels, attend_backward(): pl.pallas_call(functools.partial(attend_backward_kernel, share=share), gr...  48.4 us
    pallas_call x2, Pallas kernels, attend_forward(): pl.pallas_call(attend_forward_kernel, grid=(count,), in_specs=[SMEM, whol...  32.2 us
    all_gather x1, waiting for transfers between devices, body(): parts_all = lax.all_gather(parts, 'batch', axis=0)  20.4 us
    pallas_call x1, Pallas kernels, block_backward(): pl.pallas_call(block_backward_kernel, grid=(rows // tile,), in_specs=[SME...  19.8 us
    ppermute x12, starting transfers between devices, shift_shares(): lax.ppermute(value, 'heads', [((i + by) % shares, i) for i in range(share...  19.4 us
    pallas_call x1, Pallas kernels, block_forward(): pl.pallas_call(block_kernel, grid=(rows // tile,), in_specs=[SMEM, row, w...  17.1 us
  transfers between devices with their start and end apart: 18, of which 6 were waited for; matrix products, arithmetic and copies ran while one was open for 1% of the time, Pallas kernels for 13%

profile of v1, /device:TPU:0, one launch (start us, length us, event | category | flops | bytes accessed | tf_op | source)
XLA Modules:
  0.0 688.5 jit_solution(2083500311450652529)
XLA Ops:
  7.3 0.7 broadcast_in_dim.19
  8.0 0.7 pad.21
  8.7 0.7 pad.22
  9.3 0.7 pad.23
  10.0 1.2 concatenate.28
  11.2 3.1 collective-permute-start.3
  14.3 2.6 collective-permute-start.2
  16.9 1.3 collective-permute-start.1
  18.3 1.3 fusion.2
  19.6 0.1 fusion.1.own_ref
  19.7 0.1 pad_maximum_fusion.own_ref
  19.8 0.1 pad_dynamic-slice_fusion
  19.9 0.6 copy-done
  20.5 0.7 collective-permute-start.5
  21.3 0.3 collective-permute-start.4
  21.6 2.8 collective-permute-start
  24.4 9.3 %attend_forward.2 = (bf16[1,1024,128]{2,1,0:T(8,128)(2,1)}, bf16[1,1024,128]{2,1,0:T(8,128)(2,1)}, bf16[1,1024,128]{2,1,0:T(8,128)(2,1)}, bf16[1,3,1024,1024]{3,...) custom-call(s32[4]{0:T(128)} %length_ref.9, bf16[1024,384]{1,0:T(8,128)(2,1)} %bitcast.29, ...), custom_call_target="tpu_custom_call" | custom-call | flops 360000000 | bytes 1024 | tf_op jit(solution)/shard_map/attend_forward/pallas_call | solution.py:251
  33.8 8.3 %collective-permute-done.4 = bf16[304,384]{1,0:T(8,128)(2,1)S(1)} collective-permute-done((bf16[304,384]{1,0:T(8,128)(2,1)S(1)}, bf16[304,384]{1,0:T(8,128)(2,1)S(1)}, u32[]{:S(2)}, u32[]{:S(2)}) %collective-permute-start.4) | collective-permute-done | bytes 233504 | tf_op jit(solution)/shard_map/ppermute | solution.py:1085
  42.1 0.9 pad_maximum_fusion.1
  43.1 0.2 reduce-scatter.2.cloned.1.call-start
  43.3 0.1 collective-permute-start.6
  43.4 0.2 concatenate.29
  43.6 1.4 collective-permute-done.6
  45.1 0.1 broadcast_select_fusion
  45.2 0.9 pad_maximum_fusion.2.w_ref.w_hbm
  46.1 22.9 %attend_forward.3 = (bf16[3,1024,128]{2,1,0:T(8,128)(2,1)}, bf16[3,1024,128]{2,1,0:T(8,128)(2,1)}, bf16[3,1024,128]{2,1,0:T(8,128)(2,1)}, bf16[3,3,1024,1024]{3,...) custom-call(s32[4]{0:T(128)} %length_ref.9, bf16[1024,384]{1,0:T(8,128)(2,1)} %bitcast.30, ...), custom_call_target="tpu_custom_call" | custom-call | flops 1080000000 | bytes 1024 | tf_op jit(solution)/shard_map/attend_forward/pallas_call | solution.py:251
  69.1 0.6 pad_maximum_fusion.5.small_ref
  69.7 20.4 %all-gather.3.cloned.1.call-done = bf16[24,304,384]{2,1,0:T(8,128)(2,1)} async-done(((bf16[3,304,384]{2,1,0:T(8,128)(2,1)}), bf16[24,304,384]{2,1,0:T(8,128)(2,1)}) %all-gather.3.cloned.1.call-update) | async-done | bytes 5603344 | tf_op jit(solution)/shard_map/all_gather | solution.py:1190
  90.1 17.1 %block_forward.1 = (bf16[1024,384]{1,0:T(8,128)(2,1)}, f32[1024,384]{1,0:T(8,128)}, f32[1024,1]{1,0:T(8,128)}, f32[1024,384]{1,0:T(8,128)}, f32[1024,1]{1,0:T(8,...) custom-call(s32[4]{0:T(128)} %length_ref.9, bf16[1024,384]{1,0:T(8,128)(2,1)} %bitcast.31, ...), custom_call_target="tpu_custom_call" | custom-call | flops 800000000 | bytes 1024 | tf_op jit(solution)/shard_map/block_forward/pallas_call | solution.py:936
  107.2 361.8 %relations.1 = (f32[1024,384]{1,0:T(8,128)}, bf16[4,320,384]{2,1,0:T(8,128)(2,1)}, f32[1024,1]{1,0:T(8,128)}, f32[1,1024]{1,0:T(1,128)}) custom-call(s32[4]{0:T(128)} %length_ref.9, s32[4]{0:T(128)} %split_ref.1, bf16[1024,384]{1,0:T(8,128)(2,1)} %get-tuple-element.88.block_ref, bf16[1024,768]{1,0:T(8,128)(2,1)} %bitcast.51, bf16[1440,384]{1,0:T(8,128)(2,1)} %copy-done.1, ...), custom_call_target="tpu_custom_call" | custom-call | flops 4800000000 | bytes 1024 | tf_op jit(solution)/shard_map/relations/pallas_call | solution.py:791
  469.0 19.8 %block_backward.1 = (f32[1024,384]{1,0:T(8,128)}, bf16[1024,128]{1,0:T(8,128)(2,1)}, bf16[1024,128]{1,0:T(8,128)(2,1)}, bf16[1024,128]{1,0:T(8,128)(2,1)}, bf16[...) custom-call(s32[4]{0:T(128)} %length_ref.9, f32[1024,384]{1,0:T(8,128)} %get-tuple-element.94.d_ref, ...), custom_call_target="tpu_custom_call" | custom-call | flops 1000000000 | bytes 1024 | tf_op jit(solution)/shard_map/block_backward/pallas_call | solution.py:1046
  488.8 11.9 %attend_backward.4 = (bf16[320,384]{1,0:T(8,128)(2,1)}, f32[1024,384]{1,0:T(8,128)}) custom-call(bf16[3,1024,128]{2,1,0:T(8,128)(2,1)} %get-tuple-element.106.q_ref, bf16[3,1024,128]{2,1,0:T(8,128)(2,1)} %get-tuple-element.107.k_ref, bf16[3,1024,128]{2,1,0:T(8,128)(2,1)} %get-tuple-element.108.v_ref, bf16[3,3,1024,1024]{3,2,1,0:T(8,128)(2,1)} %get-tuple-element.109.e_hbm, ...), custom_call_target="tpu_custom_call" | custom-call | flops 400000000 | bytes 1024 | tf_op jit(solution)/shard_map/attend_backward/pallas_call | solution.py:402
  500.7 12.1 %attend_backward.5 = (bf16[320,384]{1,0:T(8,128)(2,1)}, f32[1024,384]{1,0:T(8,128)}) custom-call(bf16[3,1024,128]{2,1,0:T(8,128)(2,1)} %get-tuple-element.106.q_ref, bf16[3,1024,128]{2,1,0:T(8,128)(2,1)} %get-tuple-element.107.k_ref, bf16[3,1024,128]{2,1,0:T(8,128)(2,1)} %get-tuple-element.108.v_ref, bf16[3,3,1024,1024]{3,2,1,0:T(8,128)(2,1)} %get-tuple-element.109.e_hbm, ...), custom_call_target="tpu_custom_call" | custom-call | flops 400000000 | bytes 1024 | tf_op jit(solution)/shard_map/attend_backward/pallas_call | solution.py:402
  512.8 3.9 collective-permute-start.8
  516.7 12.3 %attend_backward.6 = (bf16[320,384]{1,0:T(8,128)(2,1)}, f32[1024,384]{1,0:T(8,128)}) custom-call(bf16[3,1024,128]{2,1,0:T(8,128)(2,1)} %get-tuple-element.106.q_ref, bf16[3,1024,128]{2,1,0:T(8,128)(2,1)} %get-tuple-element.107.k_ref, bf16[3,1024,128]{2,1,0:T(8,128)(2,1)} %get-tuple-element.108.v_ref, bf16[3,3,1024,1024]{3,2,1,0:T(8,128)(2,1)} %get-tuple-element.109.e_hbm, ...), custom_call_target="tpu_custom_call" | custom-call | flops 400000000 | bytes 1024 | tf_op jit(solution)/shard_map/attend_backward/pallas_call | solution.py:402
  529.1 12.2 %attend_backward.7 = (bf16[320,384]{1,0:T(8,128)(2,1)}, f32[1024,384]{1,0:T(8,128)}) custom-call(bf16[1,1024,128]{2,1,0:T(8,128)(2,1)} %get-tuple-element.89.q_ref, bf16[1,1024,128]{2,1,0:T(8,128)(2,1)} %get-tuple-element.90.k_ref, bf16[1,1024,128]{2,1,0:T(8,128)(2,1)} %get-tuple-element.91.v_ref, bf16[1,3,1024,1024]{3,2,1,0:T(8,128)(2,1)} %get-tuple-element.92.e_hbm, ...), custom_call_target="tpu_custom_call" | custom-call | flops 400000000 | bytes 1024 | tf_op jit(solution)/shard_map/attend_backward/pallas_call | solution.py:402
  541.3 0.7 copy-done.7
  542.0 2.1 merge.4.refs_0_
  544.2 77.7 %reduce-scatter.2.cloned.1.call-done = bf16[152,1536]{1,0:T(8,128)(2,1)} async-done(((bf16[1216,1536]{1,0:T(8,128)(2,1)}), bf16[152,1536]{1,0:T(8,128)(2,1)}) %reduce-scatter.2.cloned.1.call-update) | async-done | bytes 466960 | tf_op jit(solution)/shard_map/reduce_scatter | solution.py:1212
  621.8 1.1 fusion.3
  623.0 3.4 collective-permute-start.13
  626.4 1.1 collective-permute-start.11
  627.5 0.7 copy-done.8
  628.2 1.8 merge.5.refs_0_
  630.0 1.4 collective-permute-start.14
  631.4 5.1 collective-permute-done.12
  636.5 0.1 add_convert_fusion
  636.6 0.4 collective-permute-done.14.refs_1_
  637.1 0.7 copy-done.9
  637.7 1.8 merge.6.refs_0_
  639.6 9.5 %collective-permute-start.15 = (bf16[320,384]{1,0:T(8,128)(2,1)}, bf16[320,384]{1,0:T(8,128)(2,1)S(1)}, u32[]{:S(2)}, u32[]{:S(2)}) collective-permute-start(bf16[320,384]{1,0:T(8,128)(2,1)} %merge.6.refs_0_), channel_id=1, source_target_pairs={{0,4},{1,5},{2,6},{3,7},{4,0},{5,1},{6,2},{7,3},{8,12},{9,13},{10,... | collective-permute-start | bytes 737288 | tf_op jit(solution)/shard_map/ppermute | solution.py:1090
  649.1 13.0 %all_gather.11.rows_ref = bf16[1216,384]{1,0:T(8,128)(2,1)} all-gather(bf16[152,384]{1,0:T(8,128)(2,1)S(1)} %add_convert_fusion), channel_id=1, replica_groups=mesh['heads'=4,'batch'=8] {'batch'}, dimensions={0}, use_global_device_ids=true | all-gather | bytes 1050624 | tf_op jit(solution)/shard_map/all_gather | solution.py:1233
  662.1 2.9 finish_mid.1
  665.0 1.2 slice.69
  666.3 2.1 copy.34
  668.4 1.3 slice_reduce_fusion
  669.7 0.7 copy-done.10
  670.4 2.4 merge.7
  672.8 1.2 slice.64
  674.0 1.3 fusion.4
  675.4 1.4 fusion.5
  676.8 2.1 copy.33
  679.5 0.8 sqrt_bitcast_fusion
  680.3 1.1 pad_maximum_fusion.6
  (46 shorter events, 0.4 us)
Async XLA Ops:
  7.2 12.4 %copy-start.3 = (bf16[384,384]{1,0:T(8,128)(2,1)S(1)}, bf16[384,384]{1,0:T(8,128)(2,1)}, u32[]{:S(2)}) copy-start(bf16[384,384]{1,0:T(8,128)(2,1)} %param.29) | copy-start | bytes 884740
  7.2 12.4 %copy-start.4 = (bf16[384,384]{1,0:T(8,128)(2,1)S(1)}, bf16[384,384]{1,0:T(8,128)(2,1)}, u32[]{:S(2)}) copy-start(bf16[384,384]{1,0:T(8,128)(2,1)} %param.27) | copy-start | bytes 884740
  7.2 12.4 %copy-start.12 = (bf16[96,384]{1,0:T(8,128)(2,1)S(1)}, bf16[96,384]{1,0:T(8,128)(2,1)}, u32[]{:S(2)}) copy-start(bf16[96,384]{1,0:T(8,128)(2,1)} %param.23) | copy-start | bytes 221188
  7.2 82.9 %all-gather.3.cloned.1.call-start = ((), (), s32[]{:S(2)}) async-start(), calls=%async_computation.2 | async-start | bytes 6303744 | tf_op jit(solution)/shard_map/all_gather | solution.py:1190
  11.2 8.4 %copy-start.2 = (bf16[304,384]{1,0:T(8,128)(2,1)}, bf16[304,384]{1,0:T(8,128)(2,1)S(1)}, u32[]{:S(2)}) copy-start(bf16[304,384]{1,0:T(8,128)(2,1)S(1)} %concatenate.28) | copy-start | bytes 700420
  11.2 10.4 %collective-permute-start.3 = (bf16[152,384]{1,0:T(8,128)(2,1)S(1)}, bf16[152,384]{1,0:T(8,128)(2,1)S(1)}, u32[]{:S(2)}, u32[]{:S(2)}) collective-permute-start(bf16[152,384]{1,0:T(8,128)(2,1)S(1)} %constant_dynamic-slice_fusion), channel_id=1, source_target_pairs={{24,0},{0,8},{8,16},{16,24},{25,1},{1,9},{9,17},{17,25},{26,2},{2,... | collective-permute-start | bytes 350216 | tf_op jit(solution)/shard_map/ppermute | solution.py:1085
  14.3 19.4 %collective-permute-start.2 = (bf16[152,384]{1,0:T(8,128)(2,1)S(1)}, bf16[152,384]{1,0:T(8,128)(2,1)S(1)}, u32[]{:S(2)}, u32[]{:S(2)}) collective-permute-start(bf16[152,384]{1,0:T(8,128)(2,1)S(1)} %constant_dynamic-slice_fusion), channel_id=1, source_target_pairs={{16,0},{24,8},{0,16},{8,24},{17,1},{25,9},{1,17},{9,25},{18,2},{26... | collective-permute-start | bytes 350216 | tf_op jit(solution)/shard_map/ppermute | solution.py:1085
  16.9 16.8 %collective-permute-start.1 = (bf16[152,384]{1,0:T(8,128)(2,1)S(1)}, bf16[152,384]{1,0:T(8,128)(2,1)S(1)}, u32[]{:S(2)}, u32[]{:S(2)}) collective-permute-start(bf16[152,384]{1,0:T(8,128)(2,1)S(1)} %constant_dynamic-slice_fusion), channel_id=1, source_target_pairs={{8,0},{16,8},{24,16},{0,24},{9,1},{17,9},{25,17},{1,25},{10,2},{18... | collective-permute-start | bytes 350216 | tf_op jit(solution)/shard_map/ppermute | solution.py:1085
  18.3 1.4 copy-start.11
  19.7 0.9 copy-start
  19.8 14.0 %copy-start.1 = (bf16[1440,384]{1,0:T(8,128)(2,1)}, bf16[1440,384]{1,0:T(8,128)(2,1)S(1)}, u32[]{:S(2)}) copy-start(bf16[1440,384]{1,0:T(8,128)(2,1)S(1)} %pad_maximum_fusion.own_ref) | copy-start | bytes 3317764
  20.5 13.3 %collective-permute-start.5 = (bf16[304,384]{1,0:T(8,128)(2,1)S(1)}, bf16[304,384]{1,0:T(8,128)(2,1)S(1)}, u32[]{:S(2)}, u32[]{:S(2)}) collective-permute-start(bf16[304,384]{1,0:T(8,128)(2,1)S(1)} %pad_maximum_fusion.4), channel_id=1, source_target_pairs={{24,0},{0,8},{8,16},{16,24},{25,1},{1,9},{9,17},{17,25},{26,2},{2,... | collective-permute-start | bytes 700424 | tf_op jit(solution)/shard_map/ppermute | solution.py:1085
  21.3 20.9 %collective-permute-start.4 = (bf16[304,384]{1,0:T(8,128)(2,1)S(1)}, bf16[304,384]{1,0:T(8,128)(2,1)S(1)}, u32[]{:S(2)}, u32[]{:S(2)}) collective-permute-start(bf16[304,384]{1,0:T(8,128)(2,1)S(1)} %pad_maximum_fusion.4), channel_id=1, source_target_pairs={{16,0},{24,8},{0,16},{8,24},{17,1},{25,9},{1,17},{9,25},{18,2},{26... | collective-permute-start | bytes 700424 | tf_op jit(solution)/shard_map/ppermute | solution.py:1085
  21.6 20.5 %collective-permute-start = (bf16[304,384]{1,0:T(8,128)(2,1)S(1)}, bf16[304,384]{1,0:T(8,128)(2,1)S(1)}, u32[]{:S(2)}, u32[]{:S(2)}) collective-permute-start(bf16[304,384]{1,0:T(8,128)(2,1)S(1)} %pad_maximum_fusion.4), channel_id=1, source_target_pairs={{8,0},{16,8},{24,16},{0,24},{9,1},{17,9},{25,17},{1,25},{10,2},{18... | collective-permute-start | bytes 700424 | tf_op jit(solution)/shard_map/ppermute | solution.py:1085
  43.1 578.7 %reduce-scatter.2.cloned.1.call-start = ((), (), s32[]{:S(2)}) async-start(), calls=%async_computation.1 | async-start | bytes 4202496 | tf_op jit(solution)/shard_map/reduce_scatter | solution.py:1212
  43.3 1.7 collective-permute-start.6
  500.6 28.4 %collective-permute-start.7 = (bf16[320,384]{1,0:T(8,128)(2,1)}, bf16[320,384]{1,0:T(8,128)(2,1)S(1)}, u32[]{:S(2)}, u32[]{:S(2)}) collective-permute-start(bf16[320,384]{1,0:T(8,128)(2,1)} %get-tuple-element.114), channel_id=1, source_target_pairs={{24,0},{0,8},{8,16},{16,24},{25,1},{1,9},{9,17},{17,25},{26,2},{2,... | collective-permute-start | bytes 737288 | tf_op jit(solution)/shard_map/ppermute | solution.py:1085
  512.8 16.3 %collective-permute-start.8 = (bf16[320,384]{1,0:T(8,128)(2,1)}, bf16[320,384]{1,0:T(8,128)(2,1)S(1)}, u32[]{:S(2)}, u32[]{:S(2)}) collective-permute-start(bf16[320,384]{1,0:T(8,128)(2,1)} %get-tuple-element.117), channel_id=1, source_target_pairs={{16,0},{24,8},{0,16},{8,24},{17,1},{25,9},{1,17},{9,25},{18,2},{26... | collective-permute-start | bytes 737288 | tf_op jit(solution)/shard_map/ppermute | solution.py:1085
  529.0 12.3 %collective-permute-start.9 = (bf16[320,384]{1,0:T(8,128)(2,1)}, bf16[320,384]{1,0:T(8,128)(2,1)S(1)}, u32[]{:S(2)}, u32[]{:S(2)}) collective-permute-start(bf16[320,384]{1,0:T(8,128)(2,1)} %get-tuple-element.124), channel_id=1, source_target_pairs={{8,0},{16,8},{24,16},{0,24},{9,1},{17,9},{25,17},{1,25},{10,2},{18... | collective-permute-start | bytes 737288 | tf_op jit(solution)/shard_map/ppermute | solution.py:1085
  529.1 12.2 %copy-start.5 = (bf16[320,384]{1,0:T(8,128)(2,1)}, bf16[320,384]{1,0:T(8,128)(2,1)S(1)}, u32[]{:S(2)}) copy-start(bf16[320,384]{1,0:T(8,128)(2,1)S(1)} %collective-permute-done.7.refs_1_) | copy-start | bytes 737284
  529.1 12.2 %copy-start.6 = (bf16[320,384]{1,0:T(8,128)(2,1)}, bf16[320,384]{1,0:T(8,128)(2,1)S(1)}, u32[]{:S(2)}) copy-start(bf16[320,384]{1,0:T(8,128)(2,1)S(1)} %collective-permute-done.8.refs_2_) | copy-start | bytes 737284
  541.3 0.7 copy-start.7
  544.1 83.3 %collective-permute-start.10 = (bf16[320,384]{1,0:T(8,128)(2,1)}, bf16[320,384]{1,0:T(8,128)(2,1)S(1)}, u32[]{:S(2)}, u32[]{:S(2)}) collective-permute-start(bf16[320,384]{1,0:T(8,128)(2,1)} %merge.4.refs_0_), channel_id=1, source_target_pairs={{0,1},{1,0},{2,3},{3,2},{4,5},{5,4},{6,7},{7,6},{8,9},{9,8},{10,11... | collective-permute-start | bytes 737288 | tf_op jit(solution)/shard_map/ppermute | solution.py:1090
  623.0 8.4 %collective-permute-start.13 = (bf16[152,384]{1,0:T(8,128)(2,1)S(1)}, bf16[152,384]{1,0:T(8,128)(2,1)S(1)}, u32[]{:S(2)}, u32[]{:S(2)}) collective-permute-start(bf16[152,384]{1,0:T(8,128)(2,1)S(1)} %get-tuple-element.175), channel_id=1, source_target_pairs={{8,0},{16,8},{24,16},{0,24},{9,1},{17,9},{25,17},{1,25},{10,2},{18... | collective-permute-start | bytes 350216 | tf_op jit(solution)/shard_map/ppermute | solution.py:1085
  626.4 10.2 %collective-permute-start.12 = (bf16[152,384]{1,0:T(8,128)(2,1)S(1)}, bf16[152,384]{1,0:T(8,128)(2,1)S(1)}, u32[]{:S(2)}, u32[]{:S(2)}) collective-permute-start(bf16[152,384]{1,0:T(8,128)(2,1)S(1)} %get-tuple-element.176), channel_id=1, source_target_pairs={{16,0},{24,8},{0,16},{8,24},{17,1},{25,9},{1,17},{9,25},{18,2},{26... | collective-permute-start | bytes 350216 | tf_op jit(solution)/shard_map/ppermute | solution.py:1085
  626.4 10.2 %collective-permute-start.11 = (bf16[152,384]{1,0:T(8,128)(2,1)S(1)}, bf16[152,384]{1,0:T(8,128)(2,1)S(1)}, u32[]{:S(2)}, u32[]{:S(2)}) collective-permute-start(bf16[152,384]{1,0:T(8,128)(2,1)S(1)} %get-tuple-element.177), channel_id=1, source_target_pairs={{24,0},{0,8},{8,16},{16,24},{25,1},{1,9},{9,17},{17,25},{26,2},{2,... | collective-permute-start | bytes 350216 | tf_op jit(solution)/shard_map/ppermute | solution.py:1085
  627.5 0.7 copy-start.8
  630.0 7.1 %collective-permute-start.14 = (bf16[320,384]{1,0:T(8,128)(2,1)}, bf16[320,384]{1,0:T(8,128)(2,1)S(1)}, u32[]{:S(2)}, u32[]{:S(2)}) collective-permute-start(bf16[320,384]{1,0:T(8,128)(2,1)} %merge.5.refs_0_), channel_id=1, source_target_pairs={{0,2},{1,3},{2,0},{3,1},{4,6},{5,7},{6,4},{7,5},{8,10},{9,11},{10,... | collective-permute-start | bytes 737288 | tf_op jit(solution)/shard_map/ppermute | solution.py:1090
  637.1 0.7 copy-start.9
  639.6 30.1 %collective-permute-start.15 = (bf16[320,384]{1,0:T(8,128)(2,1)}, bf16[320,384]{1,0:T(8,128)(2,1)S(1)}, u32[]{:S(2)}, u32[]{:S(2)}) collective-permute-start(bf16[320,384]{1,0:T(8,128)(2,1)} %merge.6.refs_0_), channel_id=1, source_target_pairs={{0,4},{1,5},{2,6},{3,7},{4,0},{5,1},{6,2},{7,3},{8,12},{9,13},{10,... | collective-permute-start | bytes 737288 | tf_op jit(solution)/shard_map/ppermute | solution.py:1090
  669.7 0.7 copy-start.10
Sparse Core Ops, SparseCore 0:
  43.2 46.8 all-gather.2
  488.9 132.8 reduce-scatter.1
